TPU v7x, 32 devices: a whole 2x2x4 slice. The times are simulated.
32 devices in a mesh: dp: 8 (over z, y), mp: 4 (over x, core).
Axes of the slice: x: 2, y: 2, z: 4, core: 2. Of those that a mesh axis runs over, the one named last changes fastest.
Arguments:
- image_in: bfloat16 [512, 64, 2048], P(('dp', 'mp')), may hold values from -64 to 64
- cotangent: bfloat16 [512, 64, 2048], P(('dp', 'mp')), may hold values from -9 to 9
- heights: int32 [2, 8], replicated, may hold values from 1 to 63, as said below
- widths: int32 [2, 8], replicated, may hold values from 16 to 64, as said below
- weight_in_a: bfloat16 [2048, 512], P('dp', 'mp'), may hold values from -0.125 to 0.125
- weight_offset: bfloat16 [4608, 18], replicated, may hold values from -0.25 to 0.25
- bias_offset: float32 [18], replicated, may hold values from -3 to 3
- weight_mid_a: bfloat16 [4608, 512], P('dp', 'mp'), may hold values from -0.09375 to 0.09375
- weight_out_a: bfloat16 [512, 2048], P('dp', 'mp'), may hold values from -0.25 to 0.25
- weight_in_b: bfloat16 [2048, 512], P('dp', 'mp'), may hold values from -0.125 to 0.125
- weight_mid_b: bfloat16 [4608, 512], P('dp', 'mp'), may hold values from -0.09375 to 0.09375
- weight_out_b: bfloat16 [512, 2048], P('dp', 'mp'), may hold values from -0.25 to 0.25
- mid_gain: float32 [2, 2, 512], replicated, may hold values from 0.25 to 1.75
- mid_bias: float32 [2, 2, 512], replicated, may hold values from -3 to 3
- out_gain: float32 [2, 2048], replicated, may hold values from 0.25 to 1.75
- out_bias: float32 [2, 2048], replicated, may hold values from -3 to 3
Outputs:
- image_out: bfloat16 [512, 64, 2048], P(('dp', 'mp'))
- image_grad: float32 [512, 64, 2048], P(('dp', 'mp'))
- grad_in_a: float32 [2048, 512], P('dp', 'mp')
- grad_offset: float32 [4608, 18], replicated
- grad_offset_bias: float32 [18], replicated
- grad_mid_a: float32 [4608, 512], P('dp', 'mp')
- grad_out_a: float32 [512, 2048], P('dp', 'mp')
- grad_in_b: float32 [2048, 512], P('dp', 'mp')
- grad_mid_b: float32 [4608, 512], P('dp', 'mp')
- grad_out_b: float32 [512, 2048], P('dp', 'mp')
- grad_mid_gain: float32 [2, 2, 512], replicated
- grad_mid_bias: float32 [2, 2, 512], replicated
- grad_out_gain: float32 [2, 2048], replicated
- grad_out_bias: float32 [2, 2048], replicated
Inputs may be any that keep to these rules, and one draw needn't show every extreme that they name: Group 0's heights sum to 264 and group 1's to 248; the last image of group 0 and the first image of group 1 have exactly 63 rows. Group 0 widths lie from 32 to 64, group 1 widths from 16 to 40; in each group one image has the largest width of its range.
All inputs are finite; a program needn't handle non-finite values.
Results may differ from a plain program's by a relative error of at most 0.023.
Values may be sent and summed in bfloat16 or wider, within the bound.
A program may use at most 384 MiB of HBM per device.

v0:
```python
from functools import partial

import jax
import jax.numpy as jnp
from jax import lax
from jax.sharding import PartitionSpec as P

norm_eps = 1e-05
halo_rows = 3


def from_behind(value, axis, steps):
    count = lax.axis_size(axis)
    leading, last = (max(0, -steps), min(count, count - steps))
    return lax.ppermute(value, axis, [(source, source + steps) for source in range(leading, last)])


def extended_2(cells, sides, width):
    for axis, dim in sides:
        count = lax.axis_size(axis)
        ends = count - 1
        head = lax.slice_in_dim(cells, 0, width, axis=dim)
        tail = lax.slice_in_dim(cells, cells.shape[dim] - width, cells.shape[dim], axis=dim)
        cells = jnp.concatenate(
            [
                lax.ppermute(tail, axis, [(i, (i + 1) % count) for i in range(ends)]),
                cells,
                lax.ppermute(head, axis, [((i + 1) % count, i) for i in range(ends)]),
            ],
            axis=dim,
        )
    return cells


def gelu_tanh(values):
    return jax.nn.gelu(values, approximate=True)


def row_info(row_index, heights, widths, group_rows, total_rows):
    image_count = heights.shape[1]
    inside = (row_index >= 0) & (row_index < total_rows)
    group_of = jnp.clip(row_index // group_rows, 0, 1)
    local_row = row_index - group_of * group_rows
    image_ends = jnp.cumsum(heights, axis=1)
    is_first = (group_of == 0)[:, None]
    ends_by_row = jnp.where(is_first, image_ends[0][None, :], image_ends[1][None, :])
    image_num = jnp.sum((local_row[:, None] >= ends_by_row).astype(jnp.int32), axis=1)
    identity = jnp.where(inside, group_of * image_count + image_num, -1)
    width_table = jnp.where(is_first, widths[0][None, :], widths[1][None, :])
    picked = jnp.arange(image_count, dtype=jnp.int32)[None, :] == image_num[:, None]
    width_row = jnp.sum(jnp.where(picked, width_table, 0), axis=1)
    return (identity, jnp.where(inside, width_row, 0))


def tap_masks(identity, height):
    centre = identity[halo_rows : halo_rows + height]
    return [
        (identity[halo_rows + row_shift : halo_rows + row_shift + height] == centre).astype(
            jnp.float32
        )[:, None, None]
        for row_shift in range(-2, 4)
    ]


def window(padded, row_shift, col_shift, height, breadth):
    return padded[
        halo_rows + row_shift : halo_rows + row_shift + height,
        halo_rows + col_shift : halo_rows + col_shift + breadth,
    ]


def tap_columns(field_ext, row_masks):
    height = field_ext.shape[0] - 2 * halo_rows
    breadth = field_ext.shape[1]
    padded = jnp.pad(field_ext, ((0, 0), (halo_rows, halo_rows), (0, 0)))
    pieces = []
    for tap_row in range(3):
        for tap_col in range(3):
            row_shift = 2 * tap_row - 2
            col_shift = 2 * tap_col - 2
            pieces.append(
                row_masks[row_shift + 2] * window(padded, row_shift, col_shift, height, breadth)
            )
    return jnp.concatenate(pieces, axis=-1)


def sample_columns(field_ext, offsets, row_masks):
    height = field_ext.shape[0] - 2 * halo_rows
    breadth = field_ext.shape[1]
    padded = jnp.pad(field_ext, ((0, 0), (halo_rows, halo_rows), (0, 0)))
    pieces = []
    for tap_row in range(3):
        for tap_col in range(3):
            tap_index = 3 * tap_row + tap_col
            row_shift = 2 * tap_row - 2
            col_shift = 2 * tap_col - 2
            row_weight = offsets[:, :, 2 * tap_index][:, :, None]
            col_weight = offsets[:, :, 2 * tap_index + 1][:, :, None]
            upper_pair = (1.0 - col_weight) * window(
                padded, row_shift, col_shift, height, breadth
            ) + col_weight * window(padded, row_shift, col_shift + 1, height, breadth)
            lower_pair = (1.0 - col_weight) * window(
                padded, row_shift + 1, col_shift, height, breadth
            ) + col_weight * window(padded, row_shift + 1, col_shift + 1, height, breadth)
            pieces.append(
                (1.0 - row_weight) * row_masks[row_shift + 2] * upper_pair
                + row_weight * row_masks[row_shift + 3] * lower_pair
            )
    return jnp.concatenate(pieces, axis=-1)


def inner_rows(left_side, right_side):
    return lax.dot_general(
        left_side, right_side, (((0,), (0,)), ((), ())), preferred_element_type=jnp.float32
    )


def times_transposed(left_side, right_side):
    return lax.dot_general(
        left_side, right_side, (((1,), (1,)), ((), ())), preferred_element_type=jnp.float32
    )


def flat_dot(values, matrix):
    height, breadth = (values.shape[0], values.shape[1])
    return jnp.dot(
        values.reshape(height * breadth, -1), matrix, preferred_element_type=jnp.float32
    ).reshape(height, breadth, -1)


def gelu_back(values, valid_map, upstream):

    def gated(inner_values):
        return valid_map * gelu_tanh(inner_values)

    ignored, pullback = jax.vjp(gated, values)
    return pullback(upstream)[0]


def moments(values, valid_map, pixels):
    weighted = values * valid_map
    average = lax.psum(jnp.sum(weighted, axis=(0, 1)), ("dp", "mp")) / pixels
    centred = values - average
    spread = lax.psum(jnp.sum(centred * centred * valid_map, axis=(0, 1)), ("dp", "mp")) / pixels
    return (average, lax.rsqrt(spread + norm_eps))


def norm_back(grad_act, normed, inverse, gain_vec, valid_map, pixels, offset_terms):
    weighted = grad_act * valid_map
    bias_part = jnp.sum(weighted, axis=(0, 1))
    gain_part = jnp.sum(weighted * normed, axis=(0, 1))
    offset_sums = None
    if offset_terms is None:
        bias_grad, gain_grad = lax.psum((bias_part, gain_part), ("dp", "mp"))
    else:
        bias_grad, gain_grad, weight_sum, shift_sum = lax.psum(
            (bias_part, gain_part, offset_terms[0], offset_terms[1]), ("dp", "mp")
        )
        offset_sums = (weight_sum, shift_sum)
    grad_in = (
        valid_map
        * (gain_vec * inverse)
        * (grad_act - bias_grad / pixels - normed * gain_grad / pixels)
    )
    return (grad_in.astype(jnp.bfloat16), gain_grad, bias_grad, offset_sums)


def fold_rims(grad_ext, height):
    middle = grad_ext[halo_rows : halo_rows + height]
    for direction in (1, -1):
        if direction == 1:
            rim_piece = grad_ext[halo_rows + height :]
        else:
            rim_piece = grad_ext[:halo_rows]
        arrived = from_behind(rim_piece.astype(jnp.bfloat16), ("dp", "mp"), direction).astype(
            rim_piece.dtype
        )
        if direction == 1:
            middle = middle + jnp.pad(arrived, ((0, height - halo_rows), (0, 0), (0, 0)))
        else:
            middle = middle + jnp.pad(arrived, ((height - halo_rows, 0), (0, 0), (0, 0)))
    return middle


def full_weights(weight_in_a, weight_mid_a, weight_out_a, weight_in_b, weight_mid_b, weight_out_b):
    cols_in_a, cols_mid_a, cols_out_a, cols_in_b, cols_mid_b, cols_out_b = (
        lax.all_gather(weight_in_a, "mp", axis=1, tiled=True),
        lax.all_gather(weight_mid_a, "mp", axis=1, tiled=True),
        lax.all_gather(weight_out_a, "mp", axis=1, tiled=True),
        lax.all_gather(weight_in_b, "mp", axis=1, tiled=True),
        lax.all_gather(weight_mid_b, "mp", axis=1, tiled=True),
        lax.all_gather(weight_out_b, "mp", axis=1, tiled=True),
    )
    return tuple(
        (
            lax.all_gather(cols_in_a, "dp", axis=0, tiled=True),
            lax.all_gather(cols_mid_a, "dp", axis=0, tiled=True),
            lax.all_gather(cols_out_a, "dp", axis=0, tiled=True),
            lax.all_gather(cols_in_b, "dp", axis=0, tiled=True),
            lax.all_gather(cols_mid_b, "dp", axis=0, tiled=True),
            lax.all_gather(cols_out_b, "dp", axis=0, tiled=True),
        )
    )


def split_grads(grad_terms):
    term_in_a, term_mid_a, term_out_a, term_in_b, term_mid_b, term_out_b = grad_terms
    rows_in_a, rows_mid_a, rows_out_a, rows_in_b, rows_mid_b, rows_out_b = (
        lax.psum_scatter(term_in_a, "dp", scatter_dimension=0, tiled=True),
        lax.psum_scatter(term_mid_a, "dp", scatter_dimension=0, tiled=True),
        lax.psum_scatter(term_out_a, "dp", scatter_dimension=0, tiled=True),
        lax.psum_scatter(term_in_b, "dp", scatter_dimension=0, tiled=True),
        lax.psum_scatter(term_mid_b, "dp", scatter_dimension=0, tiled=True),
        lax.psum_scatter(term_out_b, "dp", scatter_dimension=0, tiled=True),
    )
    return tuple(
        (
            lax.psum_scatter(
                rows_in_a.astype(jnp.bfloat16), "mp", scatter_dimension=1, tiled=True
            ).astype(jnp.float32),
            lax.psum_scatter(
                rows_mid_a.astype(jnp.bfloat16), "mp", scatter_dimension=1, tiled=True
            ).astype(jnp.float32),
            lax.psum_scatter(
                rows_out_a.astype(jnp.bfloat16), "mp", scatter_dimension=1, tiled=True
            ).astype(jnp.float32),
            lax.psum_scatter(
                rows_in_b.astype(jnp.bfloat16), "mp", scatter_dimension=1, tiled=True
            ).astype(jnp.float32),
            lax.psum_scatter(
                rows_mid_b.astype(jnp.bfloat16), "mp", scatter_dimension=1, tiled=True
            ).astype(jnp.float32),
            lax.psum_scatter(
                rows_out_b.astype(jnp.bfloat16), "mp", scatter_dimension=1, tiled=True
            ).astype(jnp.float32),
        )
    )


def block_forward(
    inputs, weights, block_gain, block_bias, tail_gain, tail_bias, offset_params, geometry
):
    in_weight, mid_weight, out_weight = weights
    valid_map, row_masks, pixels = geometry
    first_out = flat_dot(inputs, in_weight)
    first_avg, first_inv = moments(first_out, valid_map, pixels)
    first_hat = (first_out - first_avg) * first_inv
    first_act = first_hat * block_gain[0] + block_bias[0]
    hidden = (valid_map * gelu_tanh(first_act)).astype(jnp.bfloat16)
    extended = extended_2(hidden, ((("dp", "mp"), 0),), halo_rows)
    ext_float = extended.astype(jnp.float32)
    columns = tap_columns(ext_float, row_masks).astype(jnp.bfloat16)
    if offset_params is None:
        raw_offset = None
        sampled = columns
    else:
        raw_offset = flat_dot(columns, offset_params[0]) + offset_params[1]
        offsets = 0.5 + 0.45 * jnp.tanh(raw_offset)
        sampled = sample_columns(ext_float, offsets, row_masks).astype(jnp.bfloat16)
    second_out = flat_dot(sampled, mid_weight)
    second_avg, second_inv = moments(second_out, valid_map, pixels)
    second_hat = (second_out - second_avg) * second_inv
    second_act = second_hat * block_gain[1] + block_bias[1]
    hidden_two = (valid_map * gelu_tanh(second_act)).astype(jnp.bfloat16)
    third_out = flat_dot(hidden_two, out_weight)
    third_avg, third_inv = moments(third_out, valid_map, pixels)
    third_hat = (third_out - third_avg) * third_inv
    total_pre = inputs.astype(jnp.float32) + (third_hat * tail_gain + tail_bias)
    result = (valid_map * gelu_tanh(total_pre)).astype(jnp.bfloat16)
    kept_state = (
        first_hat,
        first_inv,
        first_act,
        ext_float,
        columns,
        raw_offset,
        second_hat,
        second_inv,
        second_act,
        hidden_two,
        third_hat,
        third_inv,
        total_pre,
    )
    return (result, kept_state)


def block_backward(
    grad_out, inputs, weights, block_gain, tail_gain, offset_params, geometry, kept_state
):
    in_weight, mid_weight, out_weight = weights
    valid_map, row_masks, pixels = geometry
    (
        first_hat,
        first_inv,
        first_act,
        ext_float,
        columns,
        raw_offset,
        second_hat,
        second_inv,
        second_act,
        hidden_two,
        third_hat,
        third_inv,
        total_pre,
    ) = kept_state
    height, breadth = (inputs.shape[0], inputs.shape[1])
    pixel_rows = height * breadth
    grad_pre = gelu_back(total_pre, valid_map, grad_out)
    grad_third, tail_gain_grad, tail_bias_grad, unused = norm_back(
        grad_pre, third_hat, third_inv, tail_gain, valid_map, pixels, None
    )
    flat_third = grad_third.reshape(pixel_rows, -1)
    grad_out_weight = inner_rows(hidden_two.reshape(pixel_rows, -1), flat_third)
    grad_hidden_two = times_transposed(flat_third, out_weight).reshape(height, breadth, -1)
    grad_second_act = gelu_back(second_act, valid_map, grad_hidden_two)
    grad_second, mid_gain_grad, mid_bias_grad, unused = norm_back(
        grad_second_act, second_hat, second_inv, block_gain[1], valid_map, pixels, None
    )
    flat_second = grad_second.reshape(pixel_rows, -1)
    column_pull = jax.vjp(partial(tap_columns, row_masks=row_masks), ext_float)[1]
    if offset_params is None:
        grad_mid_weight = inner_rows(columns.reshape(pixel_rows, -1), flat_second)
        grad_columns = times_transposed(flat_second, mid_weight).reshape(height, breadth, -1)
        grad_ext = column_pull(grad_columns)[0]
        offset_terms = None
    else:
        tanh_raw = jnp.tanh(raw_offset)

        def sampler(field_ext, offsets):
            return sample_columns(field_ext, offsets, row_masks)

        sampled, sample_pull = jax.vjp(sampler, ext_float, 0.5 + 0.45 * tanh_raw)
        flat_sampled = sampled.astype(jnp.bfloat16).reshape(pixel_rows, -1)
        grad_mid_weight = inner_rows(flat_sampled, flat_second)
        grad_sampled = times_transposed(flat_second, mid_weight).reshape(height, breadth, -1)
        grad_ext, grad_offsets = sample_pull(grad_sampled)
        grad_raw = (grad_offsets * (0.45 * (1.0 - tanh_raw * tanh_raw))).astype(jnp.bfloat16)
        flat_raw = grad_raw.reshape(pixel_rows, -1)
        offset_terms = (
            inner_rows(columns.reshape(pixel_rows, -1), flat_raw),
            jnp.sum(flat_raw.astype(jnp.float32), axis=0),
        )
        grad_columns = times_transposed(flat_raw, offset_params[0]).reshape(height, breadth, -1)
        grad_ext = grad_ext + column_pull(grad_columns)[0]
    grad_hidden = fold_rims(grad_ext, height)
    grad_first_act = gelu_back(first_act, valid_map, grad_hidden)
    grad_first, first_gain_grad, first_bias_grad, offset_sums = norm_back(
        grad_first_act, first_hat, first_inv, block_gain[0], valid_map, pixels, offset_terms
    )
    flat_first = grad_first.reshape(pixel_rows, -1)
    grad_in_weight = inner_rows(inputs.reshape(pixel_rows, -1), flat_first)
    grad_inputs = grad_pre + times_transposed(flat_first, in_weight).reshape(height, breadth, -1)
    gain_grads = jnp.stack([first_gain_grad, mid_gain_grad])
    bias_grads = jnp.stack([first_bias_grad, mid_bias_grad])
    return (
        grad_inputs,
        (grad_in_weight, grad_mid_weight, grad_out_weight),
        gain_grads,
        bias_grads,
        tail_gain_grad,
        tail_bias_grad,
        offset_sums,
    )


def per_device(
    image_in,
    cotangent,
    heights,
    widths,
    weight_in_a,
    weight_offset,
    bias_offset,
    weight_mid_a,
    weight_out_a,
    weight_in_b,
    weight_mid_b,
    weight_out_b,
    mid_gain,
    mid_bias,
    out_gain,
    out_bias,
):
    height, breadth = (image_in.shape[0], image_in.shape[1])
    total_rows = height * lax.axis_size(("dp", "mp"))
    first_row = lax.axis_index(("dp", "mp")) * height
    row_index = first_row - halo_rows + jnp.arange(height + 2 * halo_rows, dtype=jnp.int32)
    identity, width_row = row_info(
        row_index, heights, widths, total_rows // 2 + height // 2, total_rows
    )
    row_masks = tap_masks(identity, height)
    col_index = jnp.arange(breadth, dtype=jnp.int32)
    valid_map = (col_index[None, :] < width_row[halo_rows : halo_rows + height, None]).astype(
        jnp.float32
    )[:, :, None]
    pixels = jnp.sum(heights * widths).astype(jnp.float32)
    geometry = (valid_map, row_masks, pixels)
    gathered = full_weights(
        weight_in_a, weight_mid_a, weight_out_a, weight_in_b, weight_mid_b, weight_out_b
    )
    offset_params = (weight_offset, bias_offset)
    middle_out, state_one = block_forward(
        image_in,
        gathered[0:3],
        mid_gain[0],
        mid_bias[0],
        out_gain[0],
        out_bias[0],
        offset_params,
        geometry,
    )
    image_out, state_two = block_forward(
        middle_out,
        gathered[3:6],
        mid_gain[1],
        mid_bias[1],
        out_gain[1],
        out_bias[1],
        None,
        geometry,
    )
    back_weights = full_weights(
        weight_in_a, weight_mid_a, weight_out_a, weight_in_b, weight_mid_b, weight_out_b
    )
    grad_middle, grads_two, gains_two, biases_two, tail_gain_two, tail_bias_two, unused = (
        block_backward(
            cotangent.astype(jnp.float32),
            middle_out,
            back_weights[3:6],
            mid_gain[1],
            out_gain[1],
            None,
            geometry,
            state_two,
        )
    )
    image_grad, grads_one, gains_one, biases_one, tail_gain_one, tail_bias_one, offset_sums = (
        block_backward(
            grad_middle,
            image_in,
            back_weights[0:3],
            mid_gain[0],
            out_gain[0],
            offset_params,
            geometry,
            state_one,
        )
    )
    shards = split_grads(grads_one + grads_two)
    return (
        image_out,
        image_grad,
        shards[0],
        offset_sums[0],
        offset_sums[1],
        shards[1],
        shards[2],
        shards[3],
        shards[4],
        shards[5],
        jnp.stack([gains_one, gains_two]),
        jnp.stack([biases_one, biases_two]),
        jnp.stack([tail_gain_one, tail_gain_two]),
        jnp.stack([tail_bias_one, tail_bias_two]),
    )


def solution(mesh):
    in_specs = (
        P(("dp", "mp"), None, None),
        P(("dp", "mp"), None, None),
        P(),
        P(),
        P("dp", "mp"),
        P(),
        P(),
        P("dp", "mp"),
        P("dp", "mp"),
        P("dp", "mp"),
        P("dp", "mp"),
        P("dp", "mp"),
        P(),
        P(),
        P(),
        P(),
    )
    out_specs = (
        P(("dp", "mp"), None, None),
        P(("dp", "mp"), None, None),
        P("dp", "mp"),
        P(),
        P(),
        P("dp", "mp"),
        P("dp", "mp"),
        P("dp", "mp"),
        P("dp", "mp"),
        P("dp", "mp"),
        P(),
        P(),
        P(),
        P(),
    )
    return jax.shard_map(
        per_device, mesh=mesh, in_specs=in_specs, out_specs=out_specs, check_vma=False
    )
```

profile of v0, /device:TPU:8, one launch (start us, length us, event | category | flops | bytes accessed | tf_op | source)
XLA Modules:
  0.0 1909.0 jit_solution(14610265062298715454)
XLA Ops:
  7.3 7.5 all_gather.48
  14.9 8.7 all_gather.50
  23.7 7.7 all_gather.52
  37.9 8.1 all_gather.56
  48.2 16.4 all-gather.7.cloned.1.call-done
  69.8 39.7 %psum.182 = f32[512]{0:T(512)S(1)} all-reduce(f32[512]{0:T(512)S(1)} %get-tuple-element.368), channel_id=1, replica_groups=mesh['dp'=8,'mp'=4] {'dp','mp'}, use_global_device_ids=true, to_apply=%region_4.5 | all-reduce | flops 512 | bytes 4096 | tf_op jit(solution)/shard_map/psum | solution.py:142
  109.8 42.1 %psum.183 = f32[512]{0:T(512)S(1)} all-reduce(f32[512]{0:T(512)S(1)} %multiply_reduce_fusion.72), channel_id=1, replica_groups=mesh['dp'=8,'mp'=4] {'dp','mp'}, use_global_device_ids=true, to_apply=%region_7.8 | all-reduce | flops 512 | bytes 4096 | tf_op jit(solution)/shard_map/psum | solution.py:144
  195.1 9.0 multiply_reduce_fusion.71
  204.2 40.2 %psum.184 = f32[512]{0:T(512)S(1)} all-reduce(f32[512]{0:T(512)S(1)} %get-tuple-element.372), channel_id=1, replica_groups=mesh['dp'=8,'mp'=4] {'dp','mp'}, use_global_device_ids=true, to_apply=%region_9.10 | all-reduce | flops 512 | bytes 4096 | tf_op jit(solution)/shard_map/psum | solution.py:142
  244.7 42.8 %psum.185 = f32[512]{0:T(512)S(1)} all-reduce(f32[512]{0:T(512)S(1)} %multiply_reduce_fusion.70), channel_id=1, replica_groups=mesh['dp'=8,'mp'=4] {'dp','mp'}, use_global_device_ids=true, to_apply=%region_11.12 | all-reduce | flops 512 | bytes 4096 | tf_op jit(solution)/shard_map/psum | solution.py:144
  295.0 40.7 %psum.186 = f32[2048]{0:T(1024)S(1)} all-reduce(f32[2048]{0:T(1024)S(1)} %get-tuple-element.374), channel_id=1, replica_groups=mesh['dp'=8,'mp'=4] {'dp','mp'}, use_global_device_ids=true, to_apply=%region_13.14 | all-reduce | flops 2048 | bytes 16384 | tf_op jit(solution)/shard_map/psum | solution.py:142
  340.2 41.0 %psum.187 = f32[2048]{0:T(1024)S(1)} all-reduce(f32[2048]{0:T(1024)S(1)} %multiply_reduce_fusion.4), channel_id=1, replica_groups=mesh['dp'=8,'mp'=4] {'dp','mp'}, use_global_device_ids=true, to_apply=%region_15.16 | all-reduce | flops 2048 | bytes 16384 | tf_op jit(solution)/shard_map/psum | solution.py:144
  381.2 9.0 multiply_convert_fusion.3
  395.4 39.2 %psum.188 = f32[512]{0:T(512)S(1)} all-reduce(f32[512]{0:T(512)S(1)} %get-tuple-element.376), channel_id=1, replica_groups=mesh['dp'=8,'mp'=4] {'dp','mp'}, use_global_device_ids=true, to_apply=%region_17.18 | all-reduce | flops 512 | bytes 4096 | tf_op jit(solution)/shard_map/psum | solution.py:142
  434.9 41.0 %psum.189 = f32[512]{0:T(512)S(1)} all-reduce(f32[512]{0:T(512)S(1)} %multiply_reduce_fusion.68), channel_id=1, replica_groups=mesh['dp'=8,'mp'=4] {'dp','mp'}, use_global_device_ids=true, to_apply=%region_19.20 | all-reduce | flops 512 | bytes 4096 | tf_op jit(solution)/shard_map/psum | solution.py:144
  507.5 10.0 multiply_reduce_fusion.67
  517.5 39.7 %psum.190 = f32[512]{0:T(512)S(1)} all-reduce(f32[512]{0:T(512)S(1)} %get-tuple-element.378), channel_id=1, replica_groups=mesh['dp'=8,'mp'=4] {'dp','mp'}, use_global_device_ids=true, to_apply=%region_21.22 | all-reduce | flops 512 | bytes 4096 | tf_op jit(solution)/shard_map/psum | solution.py:142
  559.1 41.1 %psum.191 = f32[512]{0:T(512)S(1)} all-reduce(f32[512]{0:T(512)S(1)} %multiply_reduce_fusion.66), channel_id=1, replica_groups=mesh['dp'=8,'mp'=4] {'dp','mp'}, use_global_device_ids=true, to_apply=%region_23.24 | all-reduce | flops 512 | bytes 4096 | tf_op jit(solution)/shard_map/psum | solution.py:144
  600.2 8.6 multiply_reduce_fusion.3
  608.8 39.2 %psum.192 = f32[2048]{0:T(1024)S(1)} all-reduce(f32[2048]{0:T(1024)S(1)} %get-tuple-element.380), channel_id=1, replica_groups=mesh['dp'=8,'mp'=4] {'dp','mp'}, use_global_device_ids=true, to_apply=%region_25.26 | all-reduce | flops 2048 | bytes 16384 | tf_op jit(solution)/shard_map/psum | solution.py:142
  652.6 41.1 %psum.193 = f32[2048]{0:T(1024)S(1)} all-reduce(f32[2048]{0:T(1024)S(1)} %multiply_reduce_fusion.2), channel_id=1, replica_groups=mesh['dp'=8,'mp'=4] {'dp','mp'}, use_global_device_ids=true, to_apply=%region_27.28 | all-reduce | flops 2048 | bytes 16384 | tf_op jit(solution)/shard_map/psum | solution.py:144
  693.7 14.9 multiply_reduce_fusion.7
  708.6 39.2 %all-reduce.83 = (f32[2048]{0:T(1024)S(1)}, f32[2048]{0:T(1024)S(1)}) all-reduce(f32[2048]{0:T(1024)S(1)} %get-tuple-element.147, f32[2048]{0:T(1024)S(1)} %get-tuple-element.146), channel_id=1, replica_groups=mesh['dp'=8,'mp'=4] {'dp','mp'}, use_global_device_ids=true, to_apply=%region_31.32 | all-reduce | flops 4096 | bytes 32768 | tf_op jit(solution)/shard_map/psum | solution.py:154
  747.7 7.3 multiply_convert_fusion.1
  762.5 8.8 multiply_reduce_fusion.77
  771.3 42.8 %all-reduce.82 = (f32[512]{0:T(512)S(1)}, f32[512]{0:T(512)S(1)}) all-reduce(f32[512]{0:T(512)S(1)} %get-tuple-element.155, f32[512]{0:T(512)S(1)} %get-tuple-element.154), channel_id=1, replica_groups=mesh['dp'=8,'mp'=4] {'dp','mp'}, use_global_device_ids=true, to_apply=%region_35.36 | all-reduce | flops 1024 | bytes 8192 | tf_op jit(solution)/shard_map/psum | solution.py:154
  817.1 11.7 fusion.12
  828.8 10.3 slice_multiply_fusion.11
  859.3 40.3 %all-reduce.81 = (f32[512]{0:T(512)S(1)}, f32[512]{0:T(512)S(1)}) all-reduce(f32[512]{0:T(512)S(1)} %get-tuple-element.153, f32[512]{0:T(512)S(1)} %get-tuple-element.152), channel_id=1, replica_groups=mesh['dp'=8,'mp'=4] {'dp','mp'}, use_global_device_ids=true, to_apply=%region_39.40 | all-reduce | flops 1024 | bytes 8192 | tf_op jit(solution)/shard_map/psum | solution.py:154
  902.3 15.1 multiply_reduce_fusion.6
  917.4 39.8 %all-reduce.80 = (f32[2048]{0:T(1024)S(1)}, f32[2048]{0:T(1024)S(1)}) all-reduce(f32[2048]{0:T(1024)S(1)} %get-tuple-element.145, f32[2048]{0:T(1024)S(1)} %get-tuple-element.144), channel_id=1, replica_groups=mesh['dp'=8,'mp'=4] {'dp','mp'}, use_global_device_ids=true, to_apply=%region_43.44 | all-reduce | flops 4096 | bytes 32768 | tf_op jit(solution)/shard_map/psum | solution.py:154
  957.3 7.3 multiply_convert_fusion
  969.8 40.4 %all-reduce.79 = (f32[512]{0:T(512)S(1)}, f32[512]{0:T(512)S(1)}) all-reduce(f32[512]{0:T(512)S(1)} %get-tuple-element.151, f32[512]{0:T(512)S(1)} %get-tuple-element.150), channel_id=1, replica_groups=mesh['dp'=8,'mp'=4] {'dp','mp'}, use_global_device_ids=true, to_apply=%region_47.48 | all-reduce | flops 1024 | bytes 8192 | tf_op jit(solution)/shard_map/psum | solution.py:154
  1107.7 21.3 %pad_add_fusion.1 = f32[22,70,512]{2,1,0:T(8,128)S(1)} fusion(f32[16,64,512]{2,1,0:T(8,128)} %get-tuple-element.210, f32[16,64,512]{2,1,0:T(8,128)} %get-tuple-element.246, f32[16,64,512]{2,1,0:T(8,128)} %get-tuple-element.245, f32[16,64,512]{2,1,0:T(8,128)} %get-tuple-element.267, f32[16,64,512]{2,1,0:T(8,128)} %get-tuple-element.238, ...), kind=kLoop, calls=%fused_computation.49 | loop fusion | flops 22865920 | bytes 66068480 | tf_op jit(solution)/shard_map/transpose(jvp())/add_any | solution.py:66
  1129.1 11.3 fusion.147
  1156.7 41.5 %all-reduce.78 = (f32[512]{0:T(512)S(1)}, f32[512]{0:T(512)S(1)}, f32[18]{0:T(128)}) all-reduce(f32[512]{0:T(512)S(1)} %get-tuple-element.149, f32[512]{0:T(512)S(1)} %get-tuple-element.148, f32[18]{0:T(128)S(1)} %get-tuple-element.171), channel_id=1, replica_groups=mesh['dp'=8,'mp'=4] {'dp','mp'}, use_global_device_ids=true, to_apply=%region_105.106 | all-reduce | flops 1042 | bytes 8336 | tf_op jit(solution)/shard_map/psum | solution.py:156
  1206.8 11.2 convolution_bitcast_fusion
  1219.3 11.3 convolution_bitcast_fusion.1
  1236.5 57.9 %reduce-scatter.19.cloned.1.call-done = f32[256,512]{0,1:T(8,128)} async-done(((f32[2048,512]{0,1:T(8,128)}), f32[256,512]{0,1:T(8,128)}) %reduce-scatter.19.cloned.1.call-update) | async-done | bytes 524304 | tf_op jit(solution)/shard_map/reduce_scatter | solution.py:209
  1296.2 163.3 %reduce-scatter.31.cloned.1.call-done = f32[576,512]{1,0:T(8,128)} async-done(((f32[4608,512]{1,0:T(8,128)}), f32[576,512]{1,0:T(8,128)}) %reduce-scatter.31.cloned.1.call-update) | async-done | bytes 1179664 | tf_op jit(solution)/shard_map/reduce_scatter | solution.py:213
  1462.1 163.5 %reduce-scatter.23.cloned.1.call-done = f32[576,512]{1,0:T(8,128)} async-done(((f32[4608,512]{1,0:T(8,128)}), f32[576,512]{1,0:T(8,128)}) %reduce-scatter.23.cloned.1.call-update) | async-done | bytes 1179664 | tf_op jit(solution)/shard_map/reduce_scatter | solution.py:210
  1636.3 9.2 convolution_add_fusion
  1650.0 21.0 %reduce-scatter.39.cloned.1.call-done = bf16[128,256]{1,0:T(8,128)(2,1)} async-done(((bf16[512,256]{1,0:T(8,128)(2,1)}), bf16[128,256]{1,0:T(8,128)(2,1)}) %reduce-scatter.39.cloned.1.call-update) | async-done | bytes 65552
  1672.6 21.3 %reduce-scatter.27.cloned.1.call-done = bf16[64,512]{1,0:T(8,128)(2,1)} async-done(((bf16[64,2048]{1,0:T(8,128)(2,1)}), bf16[64,512]{1,0:T(8,128)(2,1)}) %reduce-scatter.27.cloned.1.call-update) | async-done | bytes 65552 | tf_op jit(solution)/shard_map/reduce_scatter | solution.py:224
  1695.4 21.6 %reduce-scatter.21.cloned.1.call-done = bf16[256,128]{0,1:T(8,128)(2,1)} async-done(((bf16[256,512]{0,1:T(8,128)(2,1)}), bf16[256,128]{0,1:T(8,128)(2,1)}) %reduce-scatter.21.cloned.1.call-update) | async-done | bytes 65552 | tf_op jit(solution)/shard_map/reduce_scatter | solution.py:218
  1718.6 23.2 %reduce-scatter.41.cloned.1.call-done = bf16[128,576]{1,0:T(8,128)(2,1)} async-done(((bf16[512,576]{1,0:T(8,128)(2,1)}), bf16[128,576]{1,0:T(8,128)(2,1)}) %reduce-scatter.41.cloned.1.call-update) | async-done | bytes 147472
  1743.7 23.0 %reduce-scatter.37.cloned.1.call-done = bf16[128,576]{1,0:T(8,128)(2,1)} async-done(((bf16[512,576]{1,0:T(8,128)(2,1)}), bf16[128,576]{1,0:T(8,128)(2,1)}) %reduce-scatter.37.cloned.1.call-update) | async-done | bytes 147472
  1768.5 131.9 %all-reduce.86.cloned.1.call-done = f32[4608,18]{0,1:T(8,128)} async-done(((f32[4608,18]{0,1:T(8,128)}), f32[4608,18]{0,1:T(8,128)}) %all-reduce.86.cloned.1.call-update) | async-done | bytes 331792 | tf_op jit(solution)/shard_map/psum | solution.py:156
  (505 shorter events, 308.9 us)
Async XLA Ops:
  7.2 162.7 %copy-start = (bf16[4608,18]{0,1:T(8,128)(2,1)S(1)}, bf16[4608,18]{0,1:T(8,128)(2,1)}, u32[]{:S(2)}) copy-start(bf16[4608,18]{0,1:T(8,128)(2,1)} %param.21) | copy-start | bytes 497668
  7.2 57.3 %all-gather.7.cloned.1.call-start = ((), (), s32[]{:S(2)}) async-start(), calls=%async_computation.12 | async-start | bytes 2359296 | tf_op jit(solution)/shard_map/all_gather | solution.py:196
  14.8 33.2 %copy-start.125 = (f32[2,2,512]{2,1,0:T(2,128)S(1)}, f32[2,2,512]{2,1,0:T(2,128)}, u32[]{:S(2)}) copy-start(f32[2,2,512]{2,1,0:T(2,128)} %param.28) | copy-start | bytes 24580
  14.8 33.3 %copy-start.126 = (f32[2,2,512]{2,1,0:T(2,128)S(1)}, f32[2,2,512]{2,1,0:T(2,128)}, u32[]{:S(2)}) copy-start(f32[2,2,512]{2,1,0:T(2,128)} %param.29) | copy-start | bytes 24580
  14.8 33.3 %copy-start.115 = (f32[2,2048]{1,0:T(2,128)S(1)}, f32[2,2048]{1,0:T(2,128)}, u32[]{:S(2)}) copy-start(f32[2,2048]{1,0:T(2,128)} %param.30) | copy-start | bytes 49156
  14.8 33.3 %copy-start.116 = (f32[2,2048]{1,0:T(2,128)S(1)}, f32[2,2048]{1,0:T(2,128)}, u32[]{:S(2)}) copy-start(f32[2,2048]{1,0:T(2,128)} %param.31) | copy-start | bytes 49156
  14.8 180.3 %all-gather.9.cloned.1.call-start = ((), (), s32[]{:S(2)}) async-start(), calls=%async_computation.13 | async-start | bytes 5308416 | tf_op jit(solution)/shard_map/all_gather | solution.py:197
  23.7 264.4 %all-gather.11.cloned.1.call-start = ((), (), s32[]{:S(2)}) async-start(), calls=%async_computation.14 | async-start | bytes 2359296 | tf_op jit(solution)/shard_map/all_gather | solution.py:198
  31.4 358.7 %all-gather.13.cloned.1.call-start = ((), (), s32[]{:S(2)}) async-start(), calls=%async_computation.15 | async-start | bytes 2359296 | tf_op jit(solution)/shard_map/all_gather | solution.py:199
  37.9 469.6 %all-gather.15.cloned.1.call-start = ((), (), s32[]{:S(2)}) async-start(), calls=%async_computation.16 | async-start | bytes 5308416 | tf_op jit(solution)/shard_map/all_gather | solution.py:200
  46.1 554.2 %all-gather.17.cloned.1.call-start = ((), (), s32[]{:S(2)}) async-start(), calls=%async_computation.17 | async-start | bytes 2359296 | tf_op jit(solution)/shard_map/all_gather | solution.py:201
  48.0 104.4 %copy-start.107 = (f32[1,1,512]{2,1,0:T(1,128)}, f32[1,1,512]{2,1,0:T(1,128)S(1)}, u32[]{:S(2)}) copy-start(f32[1,1,512]{2,1,0:T(1,128)S(1)} %get-tuple-element.344) | copy-start | bytes 6148
  48.1 104.3 %copy-start.113 = (f32[1,1,512]{2,1,0:T(1,128)}, f32[1,1,512]{2,1,0:T(1,128)S(1)}, u32[]{:S(2)}) copy-start(f32[1,1,512]{2,1,0:T(1,128)S(1)} %get-tuple-element.348) | copy-start | bytes 6148
  69.8 83.7 %copy-start.5 = (f32[16,64,512]{2,1,0:T(8,128)}, f32[16,64,512]{2,1,0:T(8,128)S(1)}, u32[]{:S(2)}) copy-start(f32[16,64,512]{2,1,0:T(8,128)S(1)} %get-tuple-element.369) | copy-start | bytes 6291460
  109.5 44.0 %copy-start.99 = (f32[512]{0:T(512)}, f32[512]{0:T(512)S(1)}, u32[]{:S(2)}) copy-start(f32[512]{0:T(512)S(1)} %broadcast_divide_fusion.11) | copy-start | bytes 6148
  153.5 12.7 collective-permute-start
  155.4 11.1 collective-permute-start.1
  204.1 90.8 %copy-start.11 = (f32[16,64,512]{2,1,0:T(8,128)}, f32[16,64,512]{2,1,0:T(8,128)S(1)}, u32[]{:S(2)}) copy-start(f32[16,64,512]{2,1,0:T(8,128)S(1)} %get-tuple-element.373) | copy-start | bytes 6291460
  434.9 50.1 %copy-start.98 = (bf16[64,512]{1,0:T(8,128)(2,1)S(1)}, bf16[64,512]{1,0:T(8,128)(2,1)}, u32[]{:S(2)}) copy-start(bf16[64,512]{1,0:T(8,128)(2,1)} %param.27) | copy-start | bytes 196612
  477.6 14.6 collective-permute-start.2
  479.5 12.7 collective-permute-start.3
  492.1 738.7 %reduce-scatter.33.cloned.1.call-start = ((), (), s32[]{:S(2)}) async-start(), calls=%async_computation.26 | async-start | bytes 4718592 | tf_op jit(solution)/shard_map/reduce_scatter | solution.py:214
  762.0 470.6 %reduce-scatter.29.cloned.1.call-start = ((), (), s32[]{:S(2)}) async-start(), calls=%async_computation.24 | async-start | bytes 4718592 | tf_op jit(solution)/shard_map/reduce_scatter | solution.py:212
  845.2 8.9 collective-permute-start.4
  847.2 8.6 collective-permute-start.5
  1016.9 217.8 %reduce-scatter.25.cloned.1.call-start = ((), (), s32[]{:S(2)}) async-start(), calls=%async_computation.22 | async-start | bytes 4718592 | tf_op jit(solution)/shard_map/reduce_scatter | solution.py:211
  1028.0 42.7 %copy-start.3 = (f32[16,64,4608]{2,1,0:T(8,128)}, f32[16,64,4608]{2,1,0:T(8,128)S(1)}, u32[]{:S(2)}) copy-start(f32[16,64,4608]{2,1,0:T(8,128)S(1)} %fusion.16) | copy-start | bytes 56623108
  1081.6 212.8 %reduce-scatter.19.cloned.1.call-start = ((), (), s32[]{:S(2)}) async-start(), calls=%async_computation.18 | async-start | bytes 4718592 | tf_op jit(solution)/shard_map/reduce_scatter | solution.py:209
  1140.4 13.2 collective-permute-start.6
  1142.3 11.2 collective-permute-start.7
  1153.6 44.7 %copy-start.117 = (f32[512]{0:T(512)S(1)}, f32[512]{0:T(512)}, u32[]{:S(2)}) copy-start(f32[512]{0:T(512)} %get-tuple-element.169) | copy-start | bytes 6148
  1205.6 253.9 %reduce-scatter.31.cloned.1.call-start = ((), (), s32[]{:S(2)}) async-start(), calls=%async_computation.25 | async-start | bytes 10616832 | tf_op jit(solution)/shard_map/reduce_scatter | solution.py:213
  1218.1 407.5 %reduce-scatter.23.cloned.1.call-start = ((), (), s32[]{:S(2)}) async-start(), calls=%async_computation.21 | async-start | bytes 10616832 | tf_op jit(solution)/shard_map/reduce_scatter | solution.py:210
  1230.7 417.8 %reduce-scatter.35.cloned.1.call-start = ((), (), s32[]{:S(2)}) async-start(), calls=%async_computation.27 | async-start | bytes 327680 | tf_op jit(solution)/shard_map/reduce_scatter | solution.py:233
  1232.6 438.5 %reduce-scatter.39.cloned.1.call-start = ((), (), s32[]{:S(2)}) async-start(), calls=%async_computation.29 | async-start | bytes 327680
  1234.6 459.3 %reduce-scatter.27.cloned.1.call-start = ((), (), s32[]{:S(2)}) async-start(), calls=%async_computation.23 | async-start | bytes 327680 | tf_op jit(solution)/shard_map/reduce_scatter | solution.py:224
  1236.5 480.6 %reduce-scatter.21.cloned.1.call-start = ((), (), s32[]{:S(2)}) async-start(), calls=%async_computation.19 | async-start | bytes 327680 | tf_op jit(solution)/shard_map/reduce_scatter | solution.py:218
  1296.2 445.7 %reduce-scatter.41.cloned.1.call-start = ((), (), s32[]{:S(2)}) async-start(), calls=%async_computation.30 | async-start | bytes 819200
  1462.0 166.4 %copy-start.128 = (f32[512]{0:T(512)S(1)}, f32[512]{0:T(512)}, u32[]{:S(2)}) copy-start(f32[512]{0:T(512)} %copy-done.127) | copy-start | bytes 6148
  1462.0 166.4 %copy-start.130 = (f32[512]{0:T(512)S(1)}, f32[512]{0:T(512)}, u32[]{:S(2)}) copy-start(f32[512]{0:T(512)} %copy-done.129) | copy-start | bytes 6148
  1462.0 166.4 %copy-start.120 = (f32[512]{0:T(512)S(1)}, f32[512]{0:T(512)}, u32[]{:S(2)}) copy-start(f32[512]{0:T(512)} %copy-done.119) | copy-start | bytes 6148
  1462.0 166.4 %copy-start.122 = (f32[512]{0:T(512)S(1)}, f32[512]{0:T(512)}, u32[]{:S(2)}) copy-start(f32[512]{0:T(512)} %copy-done.121) | copy-start | bytes 6148
  1462.0 166.4 %copy-start.110 = (f32[2048]{0:T(1024)S(1)}, f32[2048]{0:T(1024)}, u32[]{:S(2)}) copy-start(f32[2048]{0:T(1024)} %copy-done.109) | copy-start | bytes 24580
  1462.0 166.4 %copy-start.112 = (f32[2048]{0:T(1024)S(1)}, f32[2048]{0:T(1024)}, u32[]{:S(2)}) copy-start(f32[2048]{0:T(1024)} %copy-done.111) | copy-start | bytes 24580
  1462.0 167.1 %copy-start.104 = (f32[2048]{0:T(1024)S(1)}, f32[2048]{0:T(1024)}, u32[]{:S(2)}) copy-start(f32[2048]{0:T(1024)} %copy-done.103) | copy-start | bytes 24580
  1462.0 167.1 %copy-start.106 = (f32[2048]{0:T(1024)S(1)}, f32[2048]{0:T(1024)}, u32[]{:S(2)}) copy-start(f32[2048]{0:T(1024)} %copy-done.105) | copy-start | bytes 24580
  1462.0 304.7 %reduce-scatter.37.cloned.1.call-start = ((), (), s32[]{:S(2)}) async-start(), calls=%async_computation.28 | async-start | bytes 819200
  1628.1 272.3 %all-reduce.86.cloned.1.call-start = ((), (), s32[]{:S(2)}) async-start(), calls=%async_computation.20 | async-start | bytes 884736 | tf_op jit(solution)/shard_map/psum | solution.py:156
  (122 other events, 1045.4 us)
Sparse Core Ops, SparseCore 0:
  15.0 49.5 all-gather.6
  66.7 79.9 all-gather.8
  148.9 49.5 all-gather.10
  200.5 48.1 all-gather.12
  250.7 79.8 all-gather.14
  492.2 50.0 all-gather.16
  762.2 90.4 reduce-scatter.32
  1017.0 88.0 reduce-scatter.28
  1108.7 90.5 reduce-scatter.24
  1205.8 88.5 reduce-scatter.18
  1298.0 161.4 reduce-scatter.30
  1463.0 162.5 reduce-scatter.22
  1628.0 20.4 reduce-scatter.34
  1650.9 20.0 reduce-scatter.38
  1673.9 19.9 reduce-scatter.26
  1697.0 20.0 reduce-scatter.20
  1719.4 22.4 reduce-scatter.40
  1744.2 22.4 reduce-scatter.36
  1772.6 127.7 all-reduce.85
where the time goes:
time: 1920 us; the launch traced here: 1910 us
  blocking collectives  777 us (40%)
  waiting for transfers between devices  660 us (34%)
  other arithmetic  242 us (13%)
  matrix products  159 us (8%)
  starting transfers between devices  31.8 us (2%)
  local copies, waits for them, and re-layouts  22 us (1%)
    psum x6, blocking collectives, moments(): lax.psum(jnp.sum(centred * centred * valid_map, axis=(0, 1)), ('dp', 'mp'))  249 us
    psum x6, blocking collectives, moments(): average = lax.psum(jnp.sum(weighted, axis=(0, 1)), ('dp', 'mp')) / pixels  239 us
    psum x5, blocking collectives, norm_back(): bias_grad, gain_grad = lax.psum((bias_part, gain_part), ('dp', 'mp'))  202 us
    reduce_scatter x1, waiting for transfers between devices, split_grads(): lax.psum_scatter(term_mid_a, 'dp', scatter_dimension=0, tiled=True)  163 us
    reduce_scatter x1, waiting for transfers between devices, split_grads(): lax.psum_scatter(term_mid_b, 'dp', scatter_dimension=0, tiled=True)  163 us
    psum x1, waiting for transfers between devices, norm_back(): lax.psum((bias_part, gain_part, offset_terms[0], offset_terms[1]), ('dp',...  132 us
    unnamed x22, waiting for transfers between devices  67.6 us
    dot_general x7, matrix products, times_transposed(): lax.dot_general(left_side, right_side, (((1,), (1,)), ((), ())), preferre...  59.8 us
  transfers between devices with their start and end apart: 27, of which 16 were waited for; matrix products, arithmetic and copies ran while one was open for 20% of the time, Pallas kernels for 0%

commit v1 on v0

--- a/solution.py
+++ b/solution.py
@@ -3,10 +3,452 @@
 import jax
 import jax.numpy as jnp
 from jax import lax
+from jax.experimental import pallas as pl
+from jax.experimental.pallas import tpu as pltpu
 from jax.sharding import PartitionSpec as P
 
 norm_eps = 1e-05
 halo_rows = 3
+MESH = pl.DeviceIdType.MESH
+f32 = jnp.float32
+bf16 = jnp.bfloat16
+
+
+class Place:
+    def __init__(self, dp_size, mp_size):
+        self.dp_size, self.mp_size = dp_size, mp_size
+        self.count = dp_size * mp_size
+        self.high = dp_size // 2
+
+    def read(self):
+        self.dp = lax.axis_index("dp")
+        self.mp = lax.axis_index("mp")
+        self.me = self.dp * self.mp_size + self.mp
+        self.z = self.dp // 2
+        self.y = lax.rem(self.dp, 2)
+        self.x = self.mp // 2
+        self.core = lax.rem(self.mp, 2)
+        return self
+
+    def at(self, linear):
+        return (linear // self.mp_size, lax.rem(linear, self.mp_size))
+
+    def core_peer(self):
+        return (self.dp, self.mp + 1 - 2 * self.core)
+
+    def x_peer(self):
+        return (self.dp, self.mp + 2 - 4 * self.x)
+
+    def y_peer(self):
+        return (self.dp + 1 - 2 * self.y, self.mp)
+
+    def z_peer(self, step):
+        return (lax.rem(self.z + step, self.high) * 2 + self.y, self.mp)
+
+
+def greet(peers):
+    barrier = pltpu.get_barrier_semaphore()
+    for peer in peers:
+        pl.semaphore_signal(barrier, inc=1, device_id=peer, device_id_type=MESH)
+    pl.semaphore_wait(barrier, len(peers))
+
+
+def remote(src, dst, send, recv, peer):
+    return pltpu.make_async_remote_copy(
+        src_ref=src,
+        dst_ref=dst,
+        send_sem=send,
+        recv_sem=recv,
+        device_id=peer,
+        device_id_type=MESH,
+    )
+
+
+def gather_kernel(sizes, *refs):
+    shards, fulls = refs[:6], refs[6:12]
+    local_sem, send_sem, recv_sem = refs[12:]
+    place = Place(*sizes).read()
+    high, z, y, x, core = place.high, place.z, place.y, place.x, place.core
+    half = high // 2
+    greet(
+        [place.z_peer(k) for k in range(1, high)]
+        + [place.x_peer(), place.y_peer(), place.core_peer()]
+    )
+
+    def cols(array, x_at, core_at):
+        width = shards[array].shape[1]
+        return pl.ds(pl.multiple_of((2 * x_at + core_at) * width, 128), width)
+
+    def stage_copies(array, stage):
+        full = fulls[array]
+        mine = cols(array, x, core)
+        lower, upper = pl.ds(0, half), pl.ds(half, high - half)
+        if stage == 0:
+            return [
+                remote(
+                    shards[array],
+                    full.at[z, y, :, mine],
+                    send_sem.at[array, k - 1],
+                    recv_sem.at[array, k - 1],
+                    place.z_peer(k),
+                )
+                for k in range(1, high)
+            ]
+        if stage == 1:
+            pairs = [
+                (full.at[lower, y, :, mine], place.x_peer()),
+                (full.at[upper, y, :, mine], place.y_peer()),
+            ]
+        elif stage == 2:
+            pairs = [
+                (full.at[lower, y, :, cols(array, 0, core)], place.y_peer()),
+                (full.at[lower, y, :, cols(array, 1, core)], place.y_peer()),
+                (full.at[upper, :, :, mine], place.x_peer()),
+            ]
+        else:
+            pairs = [
+                (full.at[:, :, :, cols(array, 0, core)], place.core_peer()),
+                (full.at[:, :, :, cols(array, 1, core)], place.core_peer()),
+            ]
+        base = high - 1 + [0, 0, 2, 5][stage]
+        return [
+            remote(ref, ref, send_sem.at[array, base + i], recv_sem.at[array, base + i], peer)
+            for i, (ref, peer) in enumerate(pairs)
+        ]
+
+    running = {}
+    for step in range(6 + 4):
+        for array in range(6):
+            stage = step - array
+            if not 0 <= stage <= 4:
+                continue
+            if stage == 0:
+                own = pltpu.make_async_copy(
+                    shards[array], fulls[array].at[z, y, :, cols(array, x, core)], local_sem.at[array]
+                )
+                own.start()
+                running[array] = [own]
+            else:
+                for copy in running[array]:
+                    copy.wait()
+                running[array] = []
+            if stage < 4:
+                copies = stage_copies(array, stage)
+                for copy in copies:
+                    copy.start()
+                running[array] = running[array] + copies
+
+
+def gather_weights(shards, sizes):
+    high = sizes[0] // 2
+    full_shapes = [
+        jax.ShapeDtypeStruct((high, 2, s.shape[0], s.shape[1] * sizes[1]), s.dtype) for s in shards
+    ]
+    anywhere = pl.BlockSpec(memory_space=pl.ANY)
+    copies = high - 1 + 7
+    fulls = pl.pallas_call(
+        partial(gather_kernel, sizes),
+        out_shape=full_shapes,
+        in_specs=[anywhere] * 6,
+        out_specs=[anywhere] * 6,
+        scratch_shapes=[
+            pltpu.SemaphoreType.DMA((6,)),
+            pltpu.SemaphoreType.DMA((6, copies)),
+            pltpu.SemaphoreType.DMA((6, copies)),
+        ],
+        compiler_params=pltpu.CompilerParams(collective_id=0, has_side_effects=True),
+        name="gather_weights",
+    )(*shards)
+    return [w.reshape(-1, w.shape[-1]) for w in fulls]
+
+
+def scatter_kernel(sizes, *refs):
+    fulls, outs = refs[:6], refs[6:12]
+    keep, from_core, from_one, from_two, from_high = [refs[12 + 6 * i : 18 + 6 * i] for i in range(5)]
+    local_sem, send_sem, recv_sem = refs[42:]
+    place = Place(*sizes).read()
+    high, z, y, x, core = place.high, place.z, place.y, place.x, place.core
+    half = high // 2
+    greet(
+        [place.z_peer(k) for k in range(1, high)]
+        + [place.x_peer(), place.y_peer(), place.core_peer()]
+    )
+
+    def cols(array, x_at, core_at):
+        width = outs[array].shape[1]
+        return pl.ds(pl.multiple_of((2 * x_at + core_at) * width, 128), width)
+
+    def copies_of(array, stage):
+        send, recv = send_sem.at[array], recv_sem.at[array]
+        kept = keep[array]
+        if stage == 0:
+            items = [
+                (fulls[array].at[:, :, :, cols(array, i, 1 - core)], from_core[array].at[i], place.core_peer())
+                for i in (0, 1)
+            ]
+        elif stage == 1:
+            first = from_one[array].at[0]
+            second = from_one[array].at[1]
+            items = []
+            for i in (0, 1):
+                items.append((kept.at[i, pl.ds(0, half), 1 - y], first.at[i], place.y_peer()))
+            for i in (0, 1):
+                items.append((kept.at[1 - x, pl.ds(half, half), i], second.at[i], place.x_peer()))
+        elif stage == 2:
+            items = [
+                (kept.at[1 - x, pl.ds(0, half), y], from_two[array].at[0], place.x_peer()),
+                (kept.at[x, pl.ds(half, half), 1 - y], from_two[array].at[1], place.y_peer()),
+            ]
+        else:
+            items = [
+                (
+                    kept.at[x, lax.rem(z + k, high), y],
+                    from_high[array].at[k - 1],
+                    place.z_peer(k),
+                )
+                for k in range(1, high)
+            ]
+        base = [0, 2, 6, 8][stage]
+        return [
+            remote(src, dst, send.at[base + i], recv.at[base + i], peer)
+            for i, (src, dst, peer) in enumerate(items)
+        ]
+
+    def add_into(target, extra):
+        target[...] = (target[...].astype(f32) + extra[...].astype(f32)).astype(bf16)
+
+    def finish(array, stage):
+        kept = keep[array]
+        if stage == 0:
+            for i in (0, 1):
+
+                def add(b, _, i=i):
+                    for c in (0, 1):
+                        add_into(kept.at[i, b, c], from_core[array].at[i, b, c])
+                    return 0
+
+                lax.fori_loop(0, high, add, 0)
+        elif stage == 1:
+
+            def add(b, _):
+                for i in (0, 1):
+                    add_into(kept.at[i, b, y], from_one[array].at[0, i, b])
+                    add_into(kept.at[x, half + b, i], from_one[array].at[1, i, b])
+                return 0
+
+            lax.fori_loop(0, half, add, 0)
+        elif stage == 2:
+
+            def add(b, _):
+                add_into(kept.at[x, b, y], from_two[array].at[0, b])
+                add_into(kept.at[x, half + b, y], from_two[array].at[1, b])
+                return 0
+
+            lax.fori_loop(0, half, add, 0)
+        else:
+            total = kept[x, z, y].astype(f32)
+            for k in range(1, high):
+                total = total + from_high[array][k - 1].astype(f32)
+            outs[array][...] = total
+
+    running = {}
+    for step in range(6 + 4):
+        for array in range(6):
+            stage = step - array
+            if not 0 <= stage <= 4:
+                continue
+            if stage == 0:
+                running[array] = [
+                    pltpu.make_async_copy(
+                        fulls[array].at[:, :, :, cols(array, i, core)],
+                        keep[array].at[i],
+                        local_sem.at[array, i],
+                    )
+                    for i in (0, 1)
+                ]
+                for copy in running[array]:
+                    copy.start()
+            else:
+                for copy in running[array]:
+                    copy.wait()
+                finish(array, stage - 1)
+                running[array] = []
+            if stage < 4:
+                copies = copies_of(array, stage)
+                for copy in copies:
+                    copy.start()
+                running[array] = running[array] + copies
+
+
+def scatter_grads(grads, sizes):
+    high, mp_size = sizes[0] // 2, sizes[1]
+    half = high // 2
+    blocked, outs = [], []
+    scratch = [[] for _ in range(5)]
+    for grad in grads:
+        rows, width = grad.shape[0] // sizes[0], grad.shape[1] // mp_size
+        blocked.append(grad.astype(bf16).reshape(high, 2, rows, grad.shape[1]))
+        outs.append(jax.ShapeDtypeStruct((rows, width), f32))
+        tile = (rows, width)
+        scratch[0].append(pltpu.VMEM((2, high, 2) + tile, bf16))
+        scratch[1].append(pltpu.VMEM((2, high, 2) + tile, bf16))
+        scratch[2].append(pltpu.VMEM((2, 2, half) + tile, bf16))
+        scratch[3].append(pltpu.VMEM((2, half) + tile, bf16))
+        scratch[4].append(pltpu.VMEM((high - 1,) + tile, bf16))
+    copies = 8 + high - 1
+    return pl.pallas_call(
+        partial(scatter_kernel, sizes),
+        out_shape=outs,
+        in_specs=[pl.BlockSpec(memory_space=pl.ANY)] * 6,
+        out_specs=[pl.BlockSpec(memory_space=pltpu.VMEM)] * 6,
+        scratch_shapes=sum(scratch, [])
+        + [
+            pltpu.SemaphoreType.DMA((6, 2)),
+            pltpu.SemaphoreType.DMA((6, copies)),
+            pltpu.SemaphoreType.DMA((6, copies)),
+        ],
+        compiler_params=pltpu.CompilerParams(
+            collective_id=1, has_side_effects=True, vmem_limit_bytes=58 * 1024 * 1024
+        ),
+        name="scatter_grads",
+    )(*blocked)
+
+
+def merge(parts, moments_mode):
+    if not moments_mode:
+        return jnp.sum(parts, axis=0)
+    pixels, sums, squares = parts[:, 0:1], parts[:, 1:2], parts[:, 2:3]
+    all_pixels, all_sums = jnp.sum(pixels, axis=0), jnp.sum(sums, axis=0)
+    apart = sums / pixels - (all_sums / all_pixels)[None]
+    all_squares = jnp.sum(squares + pixels * apart * apart, axis=0)
+    return jnp.concatenate([all_pixels, all_sums, all_squares], axis=0)
+
+
+def sync_kernel(sizes, groups, moments_mode, x_ref, o_ref, *scratch):
+    place = Place(*sizes).read()
+    me = place.me
+    barrier = pltpu.get_barrier_semaphore()
+    links = []
+    stride = 1
+    for size in groups:
+        digit = lax.rem(me // stride, size)
+        links.append((stride, size, digit))
+        stride = stride * size
+
+    def peer(link, step):
+        stride, size, digit = link
+        return place.at(me + (lax.rem(digit + step, size) - digit) * stride)
+
+    for link in links:
+
+        def greet_one(k, _, link=link):
+            pl.semaphore_signal(barrier, inc=1, device_id=peer(link, k), device_id_type=MESH)
+            return 0
+
+        lax.fori_loop(1, link[1], greet_one, 0)
+    pl.semaphore_wait(barrier, sum(size - 1 for size in groups))
+    value = x_ref[...]
+    for i, link in enumerate(links):
+        stride, size, digit = link
+        src, slots, send, recv = scratch[4 * i : 4 * i + 4]
+        src[...] = value
+
+        def push(k, _, link=link, src=src, slots=slots, send=send, recv=recv, digit=digit):
+            remote(src, slots.at[digit], send, recv, peer(link, k)).start()
+            return 0
+
+        lax.fori_loop(1, size, push, 0)
+        pltpu.make_async_copy(src, slots.at[digit], recv).start()
+        pltpu.make_async_copy(slots, slots, recv).wait()
+        rest = slots.at[pl.ds(0, size - 1)]
+        pltpu.make_async_copy(rest, rest, send).wait()
+        value = merge(slots[...], moments_mode)
+    o_ref[...] = value
+
+
+def sync(values, sizes, moments_mode=False):
+    wide = values.shape[1] > 1024
+    groups = (sizes[1], sizes[0]) if wide else (sizes[0] * sizes[1],)
+    ids = {(3, 512, True): 2, (3, 2048, True): 3, (2, 512, False): 4, (2, 2048, False): 5}
+    scratch = []
+    for size in groups:
+        scratch += [
+            pltpu.VMEM(values.shape, f32),
+            pltpu.VMEM((size,) + values.shape, f32),
+            pltpu.SemaphoreType.DMA,
+            pltpu.SemaphoreType.DMA,
+        ]
+    return pl.pallas_call(
+        partial(sync_kernel, sizes, groups, moments_mode),
+        out_shape=jax.ShapeDtypeStruct(values.shape, f32),
+        in_specs=[pl.BlockSpec(memory_space=pltpu.VMEM)],
+        out_specs=pl.BlockSpec(memory_space=pltpu.VMEM),
+        scratch_shapes=scratch,
+        compiler_params=pltpu.CompilerParams(
+            collective_id=ids[values.shape + (moments_mode,)], has_side_effects=True
+        ),
+        name="sync",
+    )(values)
+
+
+def spread_kernel(sizes, x_ref, o_ref, got, total, send, recv):
+    place = Place(*sizes).read()
+    me, count = place.me, place.count
+    barrier = pltpu.get_barrier_semaphore()
+
+    def peer(step):
+        return lax.rem(me + step, count)
+
+    def greet_one(k, _):
+        pl.semaphore_signal(barrier, inc=1, device_id=place.at(peer(k)), device_id_type=MESH)
+        return 0
+
+    lax.fori_loop(1, count, greet_one, 0)
+    pl.semaphore_wait(barrier, count - 1)
+
+    def push(k, _):
+        to = peer(k)
+        remote(x_ref.at[to], got.at[me], send.at[0], recv.at[0], place.at(to)).start()
+        return 0
+
+    lax.fori_loop(1, count, push, 0)
+    pltpu.make_async_copy(x_ref.at[me], got.at[me], recv.at[0]).start()
+    pltpu.make_async_copy(got, got, recv.at[0]).wait()
+    rest = got.at[pl.ds(0, count - 1)]
+    pltpu.make_async_copy(rest, rest, send.at[0]).wait()
+    total[...] = jnp.sum(got[...], axis=0)
+
+    def push_total(k, _):
+        remote(total, o_ref.at[me], send.at[1], recv.at[1], place.at(peer(k))).start()
+        return 0
+
+    lax.fori_loop(1, count, push_total, 0)
+    pltpu.make_async_copy(total, o_ref.at[me], recv.at[1]).start()
+    pltpu.make_async_copy(o_ref, o_ref, recv.at[1]).wait()
+    rest = o_ref.at[pl.ds(0, count - 1)]
+    pltpu.make_async_copy(rest, rest, send.at[1]).wait()
+
+
+def sum_everywhere(table, sizes):
+    count = sizes[0] * sizes[1]
+    rows, width = table.shape
+    each = 8 * (-(-rows // (8 * count)))
+    padded = jnp.pad(table, ((0, each * count - rows), (0, 0))).reshape(count, each, width)
+    whole = pl.pallas_call(
+        partial(spread_kernel, sizes),
+        out_shape=jax.ShapeDtypeStruct(padded.shape, f32),
+        in_specs=[pl.BlockSpec(memory_space=pltpu.VMEM)],
+        out_specs=pl.BlockSpec(memory_space=pltpu.VMEM),
+        scratch_shapes=[
+            pltpu.VMEM(padded.shape, f32),
+            pltpu.VMEM(padded.shape[1:], f32),
+            pltpu.SemaphoreType.DMA((2,)),
+            pltpu.SemaphoreType.DMA((2,)),
+        ],
+        compiler_params=pltpu.CompilerParams(collective_id=6, has_side_effects=True),
+        name="sum_everywhere",
+    )(padded)
+    return whole.reshape(count * each, width)[:rows]
 
 
 def from_behind(value, axis, steps):
@@ -137,32 +579,27 @@
     return pullback(upstream)[0]
 
 
-def moments(values, valid_map, pixels):
-    weighted = values * valid_map
-    average = lax.psum(jnp.sum(weighted, axis=(0, 1)), ("dp", "mp")) / pixels
-    centred = values - average
-    spread = lax.psum(jnp.sum(centred * centred * valid_map, axis=(0, 1)), ("dp", "mp")) / pixels
-    return (average, lax.rsqrt(spread + norm_eps))
-
-
-def norm_back(grad_act, normed, inverse, gain_vec, valid_map, pixels, offset_terms):
+def moments(values, valid_map, local_pixels, sizes):
+    count = jnp.full((values.shape[-1],), local_pixels)
+    total = jnp.sum(values * valid_map, axis=(0, 1))
+    centred = values - total / local_pixels
+    squares = jnp.sum(centred * centred * valid_map, axis=(0, 1))
+    merged = sync(jnp.stack([count, total, squares]), sizes, True)
+    pixels = merged[0]
+    return (merged[1] / pixels, lax.rsqrt(merged[2] / pixels + norm_eps))
+
+
+def norm_back(grad_act, normed, inverse, gain_vec, valid_map, pixels, sizes):
     weighted = grad_act * valid_map
     bias_part = jnp.sum(weighted, axis=(0, 1))
     gain_part = jnp.sum(weighted * normed, axis=(0, 1))
-    offset_sums = None
-    if offset_terms is None:
-        bias_grad, gain_grad = lax.psum((bias_part, gain_part), ("dp", "mp"))
-    else:
-        bias_grad, gain_grad, weight_sum, shift_sum = lax.psum(
-            (bias_part, gain_part, offset_terms[0], offset_terms[1]), ("dp", "mp")
-        )
-        offset_sums = (weight_sum, shift_sum)
+    bias_grad, gain_grad = sync(jnp.stack([bias_part, gain_part]), sizes)
     grad_in = (
         valid_map
         * (gain_vec * inverse)
         * (grad_act - bias_grad / pixels - normed * gain_grad / pixels)
     )
-    return (grad_in.astype(jnp.bfloat16), gain_grad, bias_grad, offset_sums)
+    return (grad_in.astype(jnp.bfloat16), gain_grad, bias_grad)
 
 
 def fold_rims(grad_ext, height):
@@ -182,68 +619,13 @@
     return middle
 
 
-def full_weights(weight_in_a, weight_mid_a, weight_out_a, weight_in_b, weight_mid_b, weight_out_b):
-    cols_in_a, cols_mid_a, cols_out_a, cols_in_b, cols_mid_b, cols_out_b = (
-        lax.all_gather(weight_in_a, "mp", axis=1, tiled=True),
-        lax.all_gather(weight_mid_a, "mp", axis=1, tiled=True),
-        lax.all_gather(weight_out_a, "mp", axis=1, tiled=True),
-        lax.all_gather(weight_in_b, "mp", axis=1, tiled=True),
-        lax.all_gather(weight_mid_b, "mp", axis=1, tiled=True),
-        lax.all_gather(weight_out_b, "mp", axis=1, tiled=True),
-    )
-    return tuple(
-        (
-            lax.all_gather(cols_in_a, "dp", axis=0, tiled=True),
-            lax.all_gather(cols_mid_a, "dp", axis=0, tiled=True),
-            lax.all_gather(cols_out_a, "dp", axis=0, tiled=True),
-            lax.all_gather(cols_in_b, "dp", axis=0, tiled=True),
-            lax.all_gather(cols_mid_b, "dp", axis=0, tiled=True),
-            lax.all_gather(cols_out_b, "dp", axis=0, tiled=True),
-        )
-    )
-
-
-def split_grads(grad_terms):
-    term_in_a, term_mid_a, term_out_a, term_in_b, term_mid_b, term_out_b = grad_terms
-    rows_in_a, rows_mid_a, rows_out_a, rows_in_b, rows_mid_b, rows_out_b = (
-        lax.psum_scatter(term_in_a, "dp", scatter_dimension=0, tiled=True),
-        lax.psum_scatter(term_mid_a, "dp", scatter_dimension=0, tiled=True),
-        lax.psum_scatter(term_out_a, "dp", scatter_dimension=0, tiled=True),
-        lax.psum_scatter(term_in_b, "dp", scatter_dimension=0, tiled=True),
-        lax.psum_scatter(term_mid_b, "dp", scatter_dimension=0, tiled=True),
-        lax.psum_scatter(term_out_b, "dp", scatter_dimension=0, tiled=True),
-    )
-    return tuple(
-        (
-            lax.psum_scatter(
-                rows_in_a.astype(jnp.bfloat16), "mp", scatter_dimension=1, tiled=True
-            ).astype(jnp.float32),
-            lax.psum_scatter(
-                rows_mid_a.astype(jnp.bfloat16), "mp", scatter_dimension=1, tiled=True
-            ).astype(jnp.float32),
-            lax.psum_scatter(
-                rows_out_a.astype(jnp.bfloat16), "mp", scatter_dimension=1, tiled=True
-            ).astype(jnp.float32),
-            lax.psum_scatter(
-                rows_in_b.astype(jnp.bfloat16), "mp", scatter_dimension=1, tiled=True
-            ).astype(jnp.float32),
-            lax.psum_scatter(
-                rows_mid_b.astype(jnp.bfloat16), "mp", scatter_dimension=1, tiled=True
-            ).astype(jnp.float32),
-            lax.psum_scatter(
-                rows_out_b.astype(jnp.bfloat16), "mp", scatter_dimension=1, tiled=True
-            ).astype(jnp.float32),
-        )
-    )
-
-
 def block_forward(
     inputs, weights, block_gain, block_bias, tail_gain, tail_bias, offset_params, geometry
 ):
     in_weight, mid_weight, out_weight = weights
-    valid_map, row_masks, pixels = geometry
+    valid_map, row_masks, pixels, local_pixels, sizes = geometry
     first_out = flat_dot(inputs, in_weight)
-    first_avg, first_inv = moments(first_out, valid_map, pixels)
+    first_avg, first_inv = moments(first_out, valid_map, local_pixels, sizes)
     first_hat = (first_out - first_avg) * first_inv
     first_act = first_hat * block_gain[0] + block_bias[0]
     hidden = (valid_map * gelu_tanh(first_act)).astype(jnp.bfloat16)
@@ -258,12 +640,12 @@
         offsets = 0.5 + 0.45 * jnp.tanh(raw_offset)
         sampled = sample_columns(ext_float, offsets, row_masks).astype(jnp.bfloat16)
     second_out = flat_dot(sampled, mid_weight)
-    second_avg, second_inv = moments(second_out, valid_map, pixels)
+    second_avg, second_inv = moments(second_out, valid_map, local_pixels, sizes)
     second_hat = (second_out - second_avg) * second_inv
     second_act = second_hat * block_gain[1] + block_bias[1]
     hidden_two = (valid_map * gelu_tanh(second_act)).astype(jnp.bfloat16)
     third_out = flat_dot(hidden_two, out_weight)
-    third_avg, third_inv = moments(third_out, valid_map, pixels)
+    third_avg, third_inv = moments(third_out, valid_map, local_pixels, sizes)
     third_hat = (third_out - third_avg) * third_inv
     total_pre = inputs.astype(jnp.float32) + (third_hat * tail_gain + tail_bias)
     result = (valid_map * gelu_tanh(total_pre)).astype(jnp.bfloat16)
@@ -289,7 +671,7 @@
     grad_out, inputs, weights, block_gain, tail_gain, offset_params, geometry, kept_state
 ):
     in_weight, mid_weight, out_weight = weights
-    valid_map, row_masks, pixels = geometry
+    valid_map, row_masks, pixels, local_pixels, sizes = geometry
     (
         first_hat,
         first_inv,
@@ -308,15 +690,15 @@
     height, breadth = (inputs.shape[0], inputs.shape[1])
     pixel_rows = height * breadth
     grad_pre = gelu_back(total_pre, valid_map, grad_out)
-    grad_third, tail_gain_grad, tail_bias_grad, unused = norm_back(
-        grad_pre, third_hat, third_inv, tail_gain, valid_map, pixels, None
+    grad_third, tail_gain_grad, tail_bias_grad = norm_back(
+        grad_pre, third_hat, third_inv, tail_gain, valid_map, pixels, sizes
     )
     flat_third = grad_third.reshape(pixel_rows, -1)
     grad_out_weight = inner_rows(hidden_two.reshape(pixel_rows, -1), flat_third)
     grad_hidden_two = times_transposed(flat_third, out_weight).reshape(height, breadth, -1)
     grad_second_act = gelu_back(second_act, valid_map, grad_hidden_two)
-    grad_second, mid_gain_grad, mid_bias_grad, unused = norm_back(
-        grad_second_act, second_hat, second_inv, block_gain[1], valid_map, pixels, None
+    grad_second, mid_gain_grad, mid_bias_grad = norm_back(
+        grad_second_act, second_hat, second_inv, block_gain[1], valid_map, pixels, sizes
     )
     flat_second = grad_second.reshape(pixel_rows, -1)
     column_pull = jax.vjp(partial(tap_columns, row_masks=row_masks), ext_float)[1]
@@ -339,16 +721,17 @@
         grad_raw = (grad_offsets * (0.45 * (1.0 - tanh_raw * tanh_raw))).astype(jnp.bfloat16)
         flat_raw = grad_raw.reshape(pixel_rows, -1)
         offset_terms = (
-            inner_rows(columns.reshape(pixel_rows, -1), flat_raw),
+            inner_rows(flat_raw, columns.reshape(pixel_rows, -1)),
             jnp.sum(flat_raw.astype(jnp.float32), axis=0),
         )
         grad_columns = times_transposed(flat_raw, offset_params[0]).reshape(height, breadth, -1)
         grad_ext = grad_ext + column_pull(grad_columns)[0]
     grad_hidden = fold_rims(grad_ext, height)
     grad_first_act = gelu_back(first_act, valid_map, grad_hidden)
-    grad_first, first_gain_grad, first_bias_grad, offset_sums = norm_back(
-        grad_first_act, first_hat, first_inv, block_gain[0], valid_map, pixels, offset_terms
-    )
+    grad_first, first_gain_grad, first_bias_grad = norm_back(
+        grad_first_act, first_hat, first_inv, block_gain[0], valid_map, pixels, sizes
+    )
+    offset_sums = offset_terms
     flat_first = grad_first.reshape(pixel_rows, -1)
     grad_in_weight = inner_rows(inputs.reshape(pixel_rows, -1), flat_first)
     grad_inputs = grad_pre + times_transposed(flat_first, in_weight).reshape(height, breadth, -1)
@@ -396,9 +779,10 @@
         jnp.float32
     )[:, :, None]
     pixels = jnp.sum(heights * widths).astype(jnp.float32)
-    geometry = (valid_map, row_masks, pixels)
-    gathered = full_weights(
-        weight_in_a, weight_mid_a, weight_out_a, weight_in_b, weight_mid_b, weight_out_b
+    sizes = (lax.axis_size("dp"), lax.axis_size("mp"))
+    geometry = (valid_map, row_masks, pixels, jnp.sum(valid_map), sizes)
+    gathered = gather_weights(
+        (weight_in_a, weight_mid_a, weight_out_a, weight_in_b, weight_mid_b, weight_out_b), sizes
     )
     offset_params = (weight_offset, bias_offset)
     middle_out, state_one = block_forward(
@@ -421,14 +805,11 @@
         None,
         geometry,
     )
-    back_weights = full_weights(
-        weight_in_a, weight_mid_a, weight_out_a, weight_in_b, weight_mid_b, weight_out_b
-    )
     grad_middle, grads_two, gains_two, biases_two, tail_gain_two, tail_bias_two, unused = (
         block_backward(
             cotangent.astype(jnp.float32),
             middle_out,
-            back_weights[3:6],
+            gathered[3:6],
             mid_gain[1],
             out_gain[1],
             None,
@@ -440,7 +821,7 @@
         block_backward(
             grad_middle,
             image_in,
-            back_weights[0:3],
+            gathered[0:3],
             mid_gain[0],
             out_gain[0],
             offset_params,
@@ -448,13 +829,19 @@
             state_one,
         )
     )
-    shards = split_grads(grads_one + grads_two)
+    shards = scatter_grads(grads_one + grads_two, sizes)
+    offset_table = jnp.concatenate(
+        [offset_sums[0].reshape(-1, 512), jnp.pad(offset_sums[1], (0, 512 - 18))[None]]
+    )
+    offset_table = sum_everywhere(offset_table, sizes)
+    offset_weight_grad = offset_table[:-1].reshape(18, -1).T
+    offset_bias_grad = offset_table[-1, :18]
     return (
         image_out,
         image_grad,
         shards[0],
-        offset_sums[0],
-        offset_sums[1],
+        offset_weight_grad,
+        offset_bias_grad,
         shards[1],
         shards[2],
         shards[3],

time: 1920 us -> 836 us (0.44)
  blocking collectives: 777 us -> 0 us
  waiting for transfers between devices: 660 us -> 5.73 us
  Pallas kernels: 0 us -> 375 us
  matrix products: 159 us -> 137 us
    psum x18 -> x0, blocking collectives: 732 us -> none  [the longest x6 249 us: moments(): lax.psum(jnp.sum(centred * centred * valid_map, axis=(0, 1)), ('dp', 'mp'))]
    reduce_scatter x9 -> x0, waiting for transfers between devices: 430 us -> none  [the longest x1 163 us: split_grads(): lax.psum_scatter(term_mid_a, 'dp', scatter_dimension=0, tiled=True)]
    pallas_call x0 -> x15, Pallas kernels: none -> 375 us  [the longest x12 151 us: sync(): pl.pallas_call(partial(sync_kernel, sizes, groups, moments_mode), out_sha...]
    psum x1 -> x0, waiting for transfers between devices: 132 us -> none  [norm_back(): lax.psum((bias_part, gain_part, offset_terms[0], offset_terms[1]), ('dp',...]
    unnamed x22 -> x0, waiting for transfers between devices: 67.6 us -> none
    all_gather x6 -> x0, blocking collectives: 45.5 us -> none  [the longest x1 8.74 us: full_weights(): lax.all_gather(weight_mid_a, 'mp', axis=1, tiled=True)]
    convert_element_type x17 -> x6, other arithmetic: 38.9 us -> 24.6 us  [norm_back(): return (grad_in.astype(jnp.bfloat16), gain_grad, bias_grad)]
  transfers between devices with their start and end apart: 27 -> 8, of which waited for: 16 -> 5; matrix products, arithmetic and copies ran while one was open for 20% -> 1% of each run, Pallas kernels for 0% -> 0%
where the time goes in v1:
time: 836 us; the launch traced here: 823 us
  Pallas kernels  375 us (45%)
  other arithmetic  243 us (29%)
  matrix products  137 us (16%)
  starting transfers between devices  29.6 us (4%)
  local copies, waits for them, and re-layouts  28.3 us (3%)
    pallas_call x12, Pallas kernels, sync(): pl.pallas_call(partial(sync_kernel, sizes, groups, moments_mode), out_sha...  151 us
    pallas_call x1, Pallas kernels, scatter_grads(): pl.pallas_call(partial(scatter_kernel, sizes), out_shape=outs, in_specs=[...  101 us
    pallas_call x1, Pallas kernels, gather_weights(): pl.pallas_call(partial(gather_kernel, sizes), out_shape=full_shapes, in_s...  94.9 us
    dot_general x7, matrix products, times_transposed(): lax.dot_general(left_side, right_side, (((1,), (1,)), ((), ())), preferre...  54.7 us
    dot_general x7, matrix products, inner_rows(): lax.dot_general(left_side, right_side, (((0,), (0,)), ((), ())), preferre...  49.4 us
    mul x7, other arithmetic, sample_columns(): col_weight * window(padded, row_shift + 1, col_shift + 1, height, breadth)  35.2 us
    dot_general x7, matrix products, flat_dot(): jnp.dot(values.reshape(height * breadth, -1), matrix, preferred_element_t...  33.3 us
    pallas_call x1, Pallas kernels, sum_everywhere(): pl.pallas_call(partial(spread_kernel, sizes), out_shape=jax.ShapeDtypeStr...  29.1 us
  transfers between devices with their start and end apart: 8, of which 5 were waited for; matrix products, arithmetic and copies ran while one was open for 1% of the time, Pallas kernels for 0%

profile of v1, /device:TPU:8, one launch (start us, length us, event | category | flops | bytes accessed | tf_op | source)
XLA Modules:
  0.0 823.4 jit_solution(12021344629091300158)
XLA Ops:
  4.8 94.9 %gather_weights.1 = (bf16[4,2,256,512]{3,2,1,0:T(8,128)(2,1)}, bf16[4,2,576,512]{3,2,1,0:T(8,128)(2,1)}, bf16[4,2,64,2048]{3,2,1,0:T(8,128)(2,1)}, bf16[4,2,256,...) custom-call(bf16[256,128]{1,0:T(8,128)(2,1)} %refs_0_.1, ...), custom_call_target="tpu_custom_call" | custom-call | tf_op jit(solution)/shard_map/gather_weights/pallas_call | solution.py:149
  99.7 6.5 multiply_reduce_fusion.73
  112.3 15.5 %sync.12 = f32[3,512]{1,0:T(4,128)} custom-call(f32[3,512]{1,0:T(4,128)} %pad_maximum_fusion.6.x_ref), custom_call_target="tpu_custom_call" | custom-call | tf_op jit(solution)/shard_map/sync/pallas_call | solution.py:381
  133.7 5.3 collective-permute-start.1
  175.2 13.2 %sync.13 = f32[3,512]{1,0:T(4,128)} custom-call(f32[3,512]{1,0:T(4,128)} %pad_maximum_fusion.7.x_ref), custom_call_target="tpu_custom_call" | custom-call | tf_op jit(solution)/shard_map/sync/pallas_call | solution.py:381
  199.4 15.2 %sync.14 = f32[3,2048]{1,0:T(4,128)} custom-call(f32[3,2048]{1,0:T(4,128)} %pad_maximum_fusion.x_ref), custom_call_target="tpu_custom_call" | custom-call | tf_op jit(solution)/shard_map/sync/pallas_call | solution.py:381
  215.5 7.7 multiply_convert_fusion.3
  227.3 12.2 %sync.15 = f32[3,512]{1,0:T(4,128)} custom-call(f32[3,512]{1,0:T(4,128)} %pad_maximum_fusion.8.x_ref), custom_call_target="tpu_custom_call" | custom-call | tf_op jit(solution)/shard_map/sync/pallas_call | solution.py:381
  244.9 5.5 collective-permute-start.3
  271.0 13.8 %sync.16 = f32[3,512]{1,0:T(4,128)} custom-call(f32[3,512]{1,0:T(4,128)} %pad_maximum_fusion.9.x_ref), custom_call_target="tpu_custom_call" | custom-call | tf_op jit(solution)/shard_map/sync/pallas_call | solution.py:381
  286.4 5.3 multiply_reduce_fusion.3
  295.6 15.3 %sync.17 = f32[3,2048]{1,0:T(4,128)} custom-call(f32[3,2048]{1,0:T(4,128)} %pad_maximum_fusion.1.x_ref), custom_call_target="tpu_custom_call" | custom-call | tf_op jit(solution)/shard_map/sync/pallas_call | solution.py:381
  311.8 14.8 %multiply_reduce_fusion.7 = (f32[2048]{0:T(1024)S(1)}, f32[2048]{0:T(1024)S(1)}, f32[16,64,2048]{2,1,0:T(8,128)}, bf16[16,64,2048]{2,1,0:T(8,128)(2,1)}) fusion(f32[16,64]{1,0:T(8,128)S(1)} %fusion.119, f32[2048]{0:T(1024)S(1)} %bitcast.328, f32[16,64,2048]{2,1,0:T(8,128)} %copy-done.4, f32[2048]{0:T(1024)S(1)} %bitcast.382, f32[2048]{0:T(1024)S(1)} %bitcast.432, ...), kind=kLoop, calls=%fused_computation.33 | loop fusion | flops 71299072 | bytes 29413376 | tf_op jit(solution)/shard_map/reduce_sum | solution.py:594
  327.3 11.2 %sync.18 = f32[2,2048]{1,0:T(2,128)} custom-call(f32[2,2048]{1,0:T(2,128)} %pad_maximum_fusion.2.x_ref), custom_call_target="tpu_custom_call" | custom-call | tf_op jit(solution)/shard_map/sync/pallas_call | solution.py:381
  339.8 7.3 multiply_convert_fusion.1
  347.1 5.2 multiply_reduce_fusion.77
  352.9 10.2 %sync.19 = f32[2,512]{1,0:T(2,128)} custom-call(f32[2,512]{1,0:T(2,128)} %pad_maximum_fusion.12.x_ref), custom_call_target="tpu_custom_call" | custom-call | tf_op jit(solution)/shard_map/sync/pallas_call | solution.py:381
  367.4 10.9 %bitcast_convert_fusion = bf16[4608,512]{1,0:T(8,128)(2,1)} fusion(bf16[16,64,4608]{2,1,0:T(8,128)(2,1)} %copy-done.79, bf16[16,64,512]{2,1,0:T(8,128)(2,1)S(1)} %multiply_convert_fusion.7), kind=kOutput, calls=%fused_computation.4 | convolution fusion | flops 4834197504 | bytes 15204352 | tf_op jit(solution)/shard_map/dot_general | solution.py:555
  378.4 9.2 %fusion.142 = f32[16,64,4608]{2,1,0:T(8,128)} fusion(bf16[16,64,512]{2,1,0:T(8,128)(2,1)S(1)} %multiply_convert_fusion.7, bf16[4608,512,1]{1,0,2:T(8,128)(2,1)S(1)} %bitcast.522), kind=kOutput, calls=%fused_computation.514 | convolution fusion | flops 4831838208 | bytes 24641536 | tf_op jit(solution)/shard_map/dot_general | solution.py:561
  387.5 9.8 %slice_multiply_fusion.11 = (f32[16,64,512]{2,1,0:T(8,128)S(1)}, f32[16,64,512]{2,1,0:T(8,128)S(1)}, f32[16,64,512]{2,1,0:T(8,128)S(1)}, f32[16,64,512]{2,1,0:T(...) fusion(f32[16,64,4608]{2,1,0:T(8,128)} %fusion.142, ...), kind=kLoop, calls=%fused_computation.149 | loop fusion | flops 3145728 | bytes 37748864 | tf_op jit(solution)/shard_map/transpose(jvp())/mul | solution.py:524
  397.4 6.2 fusion.127
  405.7 5.3 collective-permute-start.5
  411.1 6.5 bitcast_convert_fusion.2
  421.9 9.4 %sync.20 = f32[2,512]{1,0:T(2,128)} custom-call(f32[2,512]{1,0:T(2,128)} %pad_maximum_fusion.13.x_ref), custom_call_target="tpu_custom_call" | custom-call | tf_op jit(solution)/shard_map/sync/pallas_call | solution.py:381
  435.1 6.6 bitcast_convert_fusion.3
  441.7 13.5 %multiply_reduce_fusion.6 = (f32[2048]{0:T(1024)S(1)}, f32[2048]{0:T(1024)S(1)}, f32[16,64,2048]{2,1,0:T(8,128)}) fusion(f32[16,64]{1,0:T(8,128)S(1)} %fusion.119, f32[2048]{0:T(1024)S(1)} %bitcast.325, f32[16,64,2048]{2,1,0:T(8,128)S(1)} %bitcast.254, f32[2048]{0:T(1024)S(1)} %bitcast.380, f32[2048]{0:T(1024)S(1)} %bitcast.431, f32[2048]{0:T(1024)S(1)} %bitcast.388, ...), kind=kOutput, calls=%fused_computation.32 | convolution fusion | flops 2212491264 | bytes 32559104 | tf_op jit(solution)/shard_map/dot_general | solution.py:561
  456.5 11.8 %sync.21 = f32[2,2048]{1,0:T(2,128)} custom-call(f32[2,2048]{1,0:T(2,128)} %pad_maximum_fusion.3.x_ref), custom_call_target="tpu_custom_call" | custom-call | tf_op jit(solution)/shard_map/sync/pallas_call | solution.py:381
  469.7 7.3 multiply_convert_fusion
  477.0 6.1 multiply_reduce_fusion.75
  483.1 5.1 bitcast_convert_fusion.4
  489.5 9.9 %sync.22 = f32[2,512]{1,0:T(2,128)} custom-call(f32[2,512]{1,0:T(2,128)} %pad_maximum_fusion.14.x_ref), custom_call_target="tpu_custom_call" | custom-call | tf_op jit(solution)/shard_map/sync/pallas_call | solution.py:381
  503.0 10.5 %bitcast_convert_fusion.1 = bf16[4608,512]{1,0:T(8,128)(2,1)} fusion(bf16[16,64,4608]{2,1,0:T(8,128)(2,1)} %copy-done.78, bf16[16,64,512]{2,1,0:T(8,128)(2,1)S(1)} %multiply_convert_fusion.5), kind=kOutput, calls=%fused_computation.5 | convolution fusion | flops 4834197504 | bytes 15204352 | tf_op jit(solution)/shard_map/dot_general | solution.py:555
  513.5 7.1 fusion.143
  542.7 5.7 multiply_reduce_fusion.40
  548.4 5.6 fusion.79
  554.1 5.3 fusion.71
  559.4 5.6 fusion.63
  565.0 5.7 fusion.55
  570.7 5.1 fusion.75
  583.1 7.8 fusion.116
  591.9 29.1 %sum_everywhere.1 = f32[32,8,512]{2,1,0:T(8,128)} custom-call(f32[32,8,512]{2,1,0:T(8,128)} %fusion.115.x_ref), custom_call_target="tpu_custom_call" | custom-call | tf_op jit(solution)/shard_map/sum_everywhere/pallas_call | solution.py:437
  622.9 11.8 %slice_multiply_fusion.5 = (f32[16,64,512]{2,1,0:T(8,128)S(1)}, f32[16,64,512]{2,1,0:T(8,128)S(1)}, f32[16,64,512]{2,1,0:T(8,128)S(1)}, f32[16,64,512]{2,1,0:T(8...) fusion(f32[16,64,4608]{2,1,0:T(8,128)} %fusion.116, ...), kind=kLoop, calls=%fused_computation.140 | loop fusion | flops 3145728 | bytes 37748864 | tf_op jit(solution)/shard_map/transpose(jvp())/mul | solution.py:524
  637.0 20.9 %pad_add_fusion.1 = f32[22,70,512]{2,1,0:T(8,128)S(1)} fusion(f32[16,64,512]{2,1,0:T(8,128)} %get-tuple-element.175, f32[16,64,512]{2,1,0:T(8,128)} %get-tuple-element.211, f32[16,64,512]{2,1,0:T(8,128)} %get-tuple-element.210, f32[16,64,512]{2,1,0:T(8,128)} %get-tuple-element.232, f32[16,64,512]{2,1,0:T(8,128)} %get-tuple-element.203, ...), kind=kLoop, calls=%fused_computation.41 | loop fusion | flops 22865920 | bytes 66068480 | tf_op jit(solution)/shard_map/transpose(jvp())/add_any | solution.py:508
  657.9 10.7 %fusion.124 = (bf16[22,64,512]{2,1,0:T(8,128)(2,1)S(1)}, f32[22,64,512]{2,1,0:T(8,128)S(1)}) fusion(f32[16,64,512]{2,1,0:T(8,128)} %get-tuple-element.238, f32[16,64,512]{2,1,0:T(8,128)} %get-tuple-element.237, f32[16,64,512]{2,1,0:T(8,128)} %get-tuple-element.239, f32[16,64,512]{2,1,0:T(8,128)} %get-tuple-element.240, ...), kind=kLoop, calls=%fused_computation.499 | loop fusion | flops 10092544 | bytes 35258368 | tf_op jit(solution)/shard_map/convert.10
  670.8 5.3 collective-permute-start.7
  683.0 13.0 %sync.23 = f32[2,512]{1,0:T(2,128)} custom-call(f32[2,512]{1,0:T(2,128)} %pad_maximum_fusion.15.x_ref), custom_call_target="tpu_custom_call" | custom-call | tf_op jit(solution)/shard_map/sync/pallas_call | solution.py:381
  704.0 5.8 convolution_add_fusion
  712.3 100.9 %scatter_grads.1 = (f32[256,128]{1,0:T(8,128)}, f32[576,128]{1,0:T(8,128)}, f32[64,512]{1,0:T(8,128)}, f32[256,128]{1,0:T(8,128)}, f32[576,128]{1,0:T(8,128)}, /*index=5*/f32[64,512]{1,0:T(8,128)}) custom-call(bf16[4,2,256,512]{3,2,1,0:T(8,128)(2,1)} %bitcast.259, bf16[4,2,576,512]{3,2,1,0:T(8,128)(2,1)} %bitcast.261, bf16[4,2,64,2048]{3,2,1,0:T(8,128)(2,1)} %bitcast.267, ...), custom_call_target="tpu_custom_call" | custom-call | tf_op jit(solution)/shard_map/scatter_grads/pallas_call | solution.py:299
  (460 shorter events, 186.6 us)
Async XLA Ops:
  0.6 148.9 %copy-start = (bf16[4608,18]{0,1:T(8,128)(2,1)S(1)}, bf16[4608,18]{0,1:T(8,128)(2,1)}, u32[]{:S(2)}) copy-start(bf16[4608,18]{0,1:T(8,128)(2,1)} %param.21) | copy-start | bytes 497668
  4.8 125.2 %copy-start.102 = (f32[1,1,512]{2,1,0:T(1,128)}, f32[1,1,512]{2,1,0:T(1,128)S(1)}, u32[]{:S(2)}) copy-start(f32[1,1,512]{2,1,0:T(1,128)S(1)} %get-tuple-element.320) | copy-start | bytes 6148
  108.2 23.4 %copy-start.6 = (f32[1024,512]{1,0:T(8,128)}, f32[1024,512]{1,0:T(8,128)S(1)}, u32[]{:S(2)}) copy-start(f32[1024,512]{1,0:T(8,128)S(1)} %copy.34) | copy-start | bytes 6291460
  108.2 20.4 %copy-start.113 = (f32[2,2,512]{2,1,0:T(2,128)S(1)}, f32[2,2,512]{2,1,0:T(2,128)}, u32[]{:S(2)}) copy-start(f32[2,2,512]{2,1,0:T(2,128)} %param.28) | copy-start | bytes 24580
  110.9 28.1 %copy-start.104 = (f32[2,2048]{1,0:T(2,128)S(1)}, f32[2,2048]{1,0:T(2,128)}, u32[]{:S(2)}) copy-start(f32[2,2048]{1,0:T(2,128)} %param.30) | copy-start | bytes 49156
  111.0 28.1 %copy-start.105 = (f32[2,2048]{1,0:T(2,128)S(1)}, f32[2,2048]{1,0:T(2,128)}, u32[]{:S(2)}) copy-start(f32[2,2048]{1,0:T(2,128)} %param.31) | copy-start | bytes 49156
  130.0 12.4 %copy-start.100 = (f32[1,1,512]{2,1,0:T(1,128)}, f32[1,1,512]{2,1,0:T(1,128)S(1)}, u32[]{:S(2)}) copy-start(f32[1,1,512]{2,1,0:T(1,128)S(1)} %get-tuple-element.324) | copy-start | bytes 6148
  131.6 8.8 %collective-permute-start = (bf16[3,64,512]{2,1,0:T(8,128)(2,1)S(1)}, bf16[3,64,512]{2,1,0:T(8,128)(2,1)S(1)}, u32[]{:S(2)}, u32[]{:S(2)}) collective-permute-start(bf16[3,64,512]{2,1,0:T(8,128)(2,1)S(1)} %get-tuple-element.256), channel_id=1, source_target_pairs={{0,1},{1,2},{2,3},{3,4},{4,5},{5,6},{6,7},{7,8},{8,9},{9,10},{10,1... | collective-permute-start | bytes 589832 | tf_op jit(solution)/shard_map/ppermute | solution.py:468
  133.7 8.5 %collective-permute-start.1 = (bf16[3,64,512]{2,1,0:T(8,128)(2,1)S(1)}, bf16[3,64,512]{2,1,0:T(8,128)(2,1)S(1)}, u32[]{:S(2)}, u32[]{:S(2)}) collective-permute-start(bf16[3,64,512]{2,1,0:T(8,128)(2,1)S(1)} %get-tuple-element.257), channel_id=1, source_target_pairs={{1,0},{2,1},{3,2},{4,3},{5,4},{6,5},{7,6},{8,7},{9,8},{10,9},{11,1... | collective-permute-start | bytes 589832 | tf_op jit(solution)/shard_map/ppermute | solution.py:470
  139.7 15.0 %copy-start.117 = (f32[16]{0:T(128)}, f32[16]{0:T(128)S(1)}, u32[]{:S(2)}) copy-start(f32[16]{0:T(128)S(1)} %get-tuple-element.350) | copy-start | bytes 196
  139.7 16.0 %copy-start.119 = (f32[16]{0:T(128)}, f32[16]{0:T(128)S(1)}, u32[]{:S(2)}) copy-start(f32[16]{0:T(128)S(1)} %get-tuple-element.351) | copy-start | bytes 196
  139.7 16.0 %copy-start.121 = (f32[16]{0:T(128)}, f32[16]{0:T(128)S(1)}, u32[]{:S(2)}) copy-start(f32[16]{0:T(128)S(1)} %get-tuple-element.352) | copy-start | bytes 196
  142.4 24.6 %copy-start.1 = (f32[22,64,512]{2,1,0:T(8,128)}, f32[22,64,512]{2,1,0:T(8,128)S(1)}, u32[]{:S(2)}) copy-start(f32[22,64,512]{2,1,0:T(8,128)S(1)} %maximum_convert_fusion) | copy-start | bytes 8650756
  155.7 10.1 %copy-start.70 = (f32[16,64,1]{1,2,0:T(1,128)}, f32[16,64,1]{1,2,0:T(1,128)S(1)}, u32[]{:S(2)}) copy-start(f32[16,64,1]{1,2,0:T(1,128)S(1)} %get-tuple-element.290) | copy-start | bytes 12292
  155.7 10.1 %copy-start.92 = (f32[16,64,1]{1,2,0:T(1,128)}, f32[16,64,1]{1,2,0:T(1,128)S(1)}, u32[]{:S(2)}) copy-start(f32[16,64,1]{1,2,0:T(1,128)S(1)} %get-tuple-element.259) | copy-start | bytes 12292
  155.7 11.3 %copy-start.60 = (f32[16,64,1]{1,2,0:T(1,128)}, f32[16,64,1]{1,2,0:T(1,128)S(1)}, u32[]{:S(2)}) copy-start(f32[16,64,1]{1,2,0:T(1,128)S(1)} %get-tuple-element.258) | copy-start | bytes 12292
  155.7 11.3 %copy-start.62 = (f32[16,64,1]{1,2,0:T(1,128)}, f32[16,64,1]{1,2,0:T(1,128)S(1)}, u32[]{:S(2)}) copy-start(f32[16,64,1]{1,2,0:T(1,128)S(1)} %get-tuple-element.292) | copy-start | bytes 12292
  156.0 9.8 %copy-start.56 = (f32[16,64,1]{1,2,0:T(1,128)}, f32[16,64,1]{1,2,0:T(1,128)S(1)}, u32[]{:S(2)}) copy-start(f32[16,64,1]{1,2,0:T(1,128)S(1)} %get-tuple-element.281) | copy-start | bytes 12292
  156.0 9.8 %copy-start.58 = (f32[16,64,1]{1,2,0:T(1,128)}, f32[16,64,1]{1,2,0:T(1,128)S(1)}, u32[]{:S(2)}) copy-start(f32[16,64,1]{1,2,0:T(1,128)S(1)} %get-tuple-element.289) | copy-start | bytes 12292
  156.0 11.0 %copy-start.80 = (f32[16,64,1]{1,2,0:T(1,128)}, f32[16,64,1]{1,2,0:T(1,128)S(1)}, u32[]{:S(2)}) copy-start(f32[16,64,1]{1,2,0:T(1,128)S(1)} %get-tuple-element.273) | copy-start | bytes 12292
  156.0 11.0 %copy-start.82 = (f32[16,64,1]{1,2,0:T(1,128)}, f32[16,64,1]{1,2,0:T(1,128)S(1)}, u32[]{:S(2)}) copy-start(f32[16,64,1]{1,2,0:T(1,128)S(1)} %get-tuple-element.288) | copy-start | bytes 12292
  173.5 21.7 %copy-start.11 = (f32[16,64,512]{2,1,0:T(8,128)}, f32[16,64,512]{2,1,0:T(8,128)S(1)}, u32[]{:S(2)}) copy-start(f32[16,64,512]{2,1,0:T(8,128)S(1)} %get-tuple-element.360) | copy-start | bytes 6291460
  226.6 23.8 %copy-start.123 = (s32[2,8]{1,0:T(2,128)S(1)}, s32[2,8]{1,0:T(2,128)}, u32[]{:S(2)}) copy-start(s32[2,8]{1,0:T(2,128)} %param.18) | copy-start | bytes 196
  226.6 23.8 %copy-start.124 = (s32[2,8]{1,0:T(2,128)S(1)}, s32[2,8]{1,0:T(2,128)}, u32[]{:S(2)}) copy-start(s32[2,8]{1,0:T(2,128)} %param.19) | copy-start | bytes 196
  242.8 9.1 %collective-permute-start.2 = (bf16[3,64,512]{2,1,0:T(8,128)(2,1)}, bf16[3,64,512]{2,1,0:T(8,128)(2,1)}, u32[]{:S(2)}, u32[]{:S(2)}) collective-permute-start(bf16[3,64,512]{2,1,0:T(8,128)(2,1)} %get-tuple-element.254), channel_id=1, source_target_pairs={{0,1},{1,2},{2,3},{3,4},{4,5},{5,6},{6,7},{7,8},{8,9},{9,10},{10,1... | collective-permute-start | bytes 589832 | tf_op jit(solution)/shard_map/ppermute | solution.py:468
  244.9 8.8 %collective-permute-start.3 = (bf16[3,64,512]{2,1,0:T(8,128)(2,1)}, bf16[3,64,512]{2,1,0:T(8,128)(2,1)}, u32[]{:S(2)}, u32[]{:S(2)}) collective-permute-start(bf16[3,64,512]{2,1,0:T(8,128)(2,1)} %get-tuple-element.255), channel_id=1, source_target_pairs={{1,0},{2,1},{3,2},{4,3},{5,4},{6,5},{7,6},{8,7},{9,8},{10,9},{11,1... | collective-permute-start | bytes 589832 | tf_op jit(solution)/shard_map/ppermute | solution.py:470
  364.4 13.9 %slice-start.10 = ((s8[4718592]{0:T(1024)(128)(4,1)}), s8[4194304]{0:T(1024)(128)(4,1)S(1)}, s32[]{:S(2)}) async-start(s8[4718592]{0:T(1024)(128)(4,1)} %bitcast.520), calls=%async_computation.10 | async-start | bytes 8388608
  367.4 10.9 %slice-start.11 = ((s8[4718592]{0:T(1024)(128)(4,1)}), s8[524288]{0:T(1024)(128)(4,1)S(1)}, s32[]{:S(2)}) async-start(s8[4718592]{0:T(1024)(128)(4,1)} %bitcast.520), calls=%async_computation.11 | async-start | bytes 1048576
  397.4 13.7 %copy-start.15 = (f32[16,64,512]{2,1,0:T(8,128)S(1)}, f32[16,64,512]{2,1,0:T(8,128)}, u32[]{:S(2)}) copy-start(f32[16,64,512]{2,1,0:T(8,128)} %copy-done.13) | copy-start | bytes 6291460
  403.7 13.9 %collective-permute-start.4 = (bf16[3,64,512]{2,1,0:T(8,128)(2,1)S(1)}, bf16[3,64,512]{2,1,0:T(8,128)(2,1)S(1)}, u32[]{:S(2)}, u32[]{:S(2)}) collective-permute-start(bf16[3,64,512]{2,1,0:T(8,128)(2,1)S(1)} %get-tuple-element.250), channel_id=1, source_target_pairs={{0,1},{1,2},{2,3},{3,4},{4,5},{5,6},{6,7},{7,8},{8,9},{9,10},{10,1... | collective-permute-start | bytes 589832 | tf_op jit(solution)/shard_map/ppermute | solution.py:457
  405.7 11.8 %collective-permute-start.5 = (bf16[3,64,512]{2,1,0:T(8,128)(2,1)S(1)}, bf16[3,64,512]{2,1,0:T(8,128)(2,1)S(1)}, u32[]{:S(2)}, u32[]{:S(2)}) collective-permute-start(bf16[3,64,512]{2,1,0:T(8,128)(2,1)S(1)} %get-tuple-element.251), channel_id=1, source_target_pairs={{1,0},{2,1},{3,2},{4,3},{5,4},{6,5},{7,6},{8,7},{9,8},{10,9},{11,1... | collective-permute-start | bytes 589832 | tf_op jit(solution)/shard_map/ppermute | solution.py:457
  432.7 9.0 %slice-start.2 = ((s8[8388608]{0:T(1024)(128)(4,1)}), s8[4194304]{0:T(1024)(128)(4,1)S(1)}, s32[]{:S(2)}) async-start(s8[8388608]{0:T(1024)(128)(4,1)} %bitcast.255), calls=%async_computation.2 | async-start | bytes 8388608
  483.1 17.6 %copy-start.110 = (f32[1,1,512]{2,1,0:T(1,128)S(1)}, f32[1,1,512]{2,1,0:T(1,128)}, u32[]{:S(2)}) copy-start(f32[1,1,512]{2,1,0:T(1,128)} %get-tuple-element.145) | copy-start | bytes 6148
  657.8 18.2 %copy-start.114 = (f32[1,512]{1,0:T(1,128)S(1)}, f32[1,512]{1,0:T(1,128)}, u32[]{:S(2)}) copy-start(f32[1,512]{1,0:T(1,128)} %get-tuple-element.334) | copy-start | bytes 6148
  657.8 18.2 %copy-start.116 = (f32[1,512]{1,0:T(1,128)S(1)}, f32[1,512]{1,0:T(1,128)}, u32[]{:S(2)}) copy-start(f32[1,512]{1,0:T(1,128)} %get-tuple-element.331) | copy-start | bytes 6148
  657.9 18.2 %copy-start.98 = (f32[1,2048]{1,0:T(1,128)S(1)}, f32[1,2048]{1,0:T(1,128)}, u32[]{:S(2)}) copy-start(f32[1,2048]{1,0:T(1,128)} %get-tuple-element.310) | copy-start | bytes 24580
  657.9 18.2 %copy-start.99 = (f32[1,2048]{1,0:T(1,128)S(1)}, f32[1,2048]{1,0:T(1,128)}, u32[]{:S(2)}) copy-start(f32[1,2048]{1,0:T(1,128)} %get-tuple-element.307) | copy-start | bytes 24580
  657.9 21.4 %copy-start.7 = (f32[1024,512]{1,0:T(8,128)S(1)}, f32[1024,512]{1,0:T(8,128)}, u32[]{:S(2)}) copy-start(f32[1024,512]{1,0:T(8,128)} %copy-done.6) | copy-start | bytes 6291460
  657.9 21.3 %copy-start.95 = (f32[1,512]{1,0:T(1,128)S(1)}, f32[1,512]{1,0:T(1,128)}, u32[]{:S(2)}) copy-start(f32[1,512]{1,0:T(1,128)} %copy-done.94) | copy-start | bytes 6148
  657.9 21.3 %copy-start.97 = (f32[1,512]{1,0:T(1,128)S(1)}, f32[1,512]{1,0:T(1,128)}, u32[]{:S(2)}) copy-start(f32[1,512]{1,0:T(1,128)} %copy-done.96) | copy-start | bytes 6148
  657.9 21.3 %copy-start.101 = (f32[1,1,512]{2,1,0:T(1,128)S(1)}, f32[1,1,512]{2,1,0:T(1,128)}, u32[]{:S(2)}) copy-start(f32[1,1,512]{2,1,0:T(1,128)} %copy-done.100) | copy-start | bytes 6148
  657.9 21.3 %copy-start.103 = (f32[1,1,512]{2,1,0:T(1,128)S(1)}, f32[1,1,512]{2,1,0:T(1,128)}, u32[]{:S(2)}) copy-start(f32[1,1,512]{2,1,0:T(1,128)} %copy-done.102) | copy-start | bytes 6148
  668.7 9.2 %collective-permute-start.6 = (bf16[3,64,512]{2,1,0:T(8,128)(2,1)S(1)}, bf16[3,64,512]{2,1,0:T(8,128)(2,1)S(1)}, u32[]{:S(2)}, u32[]{:S(2)}) collective-permute-start(bf16[3,64,512]{2,1,0:T(8,128)(2,1)S(1)} %get-tuple-element.252), channel_id=1, source_target_pairs={{0,1},{1,2},{2,3},{3,4},{4,5},{5,6},{6,7},{7,8},{8,9},{9,10},{10,1... | collective-permute-start | bytes 589832 | tf_op jit(solution)/shard_map/ppermute | solution.py:457
  670.8 8.5 %collective-permute-start.7 = (bf16[3,64,512]{2,1,0:T(8,128)(2,1)S(1)}, bf16[3,64,512]{2,1,0:T(8,128)(2,1)S(1)}, u32[]{:S(2)}, u32[]{:S(2)}) collective-permute-start(bf16[3,64,512]{2,1,0:T(8,128)(2,1)S(1)} %get-tuple-element.253), channel_id=1, source_target_pairs={{1,0},{2,1},{3,2},{4,3},{5,4},{6,5},{7,6},{8,7},{9,8},{10,9},{11,1... | collective-permute-start | bytes 589832 | tf_op jit(solution)/shard_map/ppermute | solution.py:457
  679.2 17.6 %copy-start.109 = (f32[1,1,512]{2,1,0:T(1,128)S(1)}, f32[1,1,512]{2,1,0:T(1,128)}, u32[]{:S(2)}) copy-start(f32[1,1,512]{2,1,0:T(1,128)} %get-tuple-element.140) | copy-start | bytes 6148
  712.3 100.9 %copy-start.115 = (f32[1,512]{1,0:T(1,128)S(1)}, f32[1,512]{1,0:T(1,128)}, u32[]{:S(2)}) copy-start(f32[1,512]{1,0:T(1,128)} %get-tuple-element.328) | copy-start | bytes 6148
  712.3 101.5 %copy-start.106 = (f32[1,2,512]{2,1,0:T(2,128)S(1)}, f32[1,2,512]{2,1,0:T(2,128)}, u32[]{:S(2)}) copy-start(f32[1,2,512]{2,1,0:T(2,128)} %maximum_bitcast_fusion.1) | copy-start | bytes 12292
  813.2 9.3 %copy-start.51 = (f32[64,512]{1,0:T(8,128)S(1)}, f32[64,512]{1,0:T(8,128)}, u32[]{:S(2)}) copy-start(f32[64,512]{1,0:T(8,128)} %get-tuple-element.397) | copy-start | bytes 393220
  (103 other events, 525.1 us)

commit v2 on v0

v2 whole, which is shorter than its diff:
```python
from functools import partial
from types import SimpleNamespace

import jax
import jax.numpy as jnp
from jax import lax
from jax.experimental import pallas as pl
from jax.experimental.pallas import tpu as pltpu
from jax.sharding import PartitionSpec as P

norm_eps = 1e-05
halo_rows = 3
breadth = 64
chunk = 256
strip = 16
lane_block = 512
offsets_count = 18
gelu_a = 0.7978845608028654
gelu_b = gelu_a * 0.044715
MESH = pl.DeviceIdType.MESH
f32 = jnp.float32
bf16 = jnp.bfloat16
shape = jax.ShapeDtypeStruct
dma = pltpu.SemaphoreType.DMA
vmem = pl.BlockSpec(memory_space=pltpu.VMEM)
smem = pl.BlockSpec(memory_space=pltpu.SMEM)
anywhere = pl.BlockSpec(memory_space=pl.ANY)


class Place:
    def __init__(self, dp_size, mp_size):
        self.dp_size, self.mp_size = dp_size, mp_size
        self.count = dp_size * mp_size
        self.high = dp_size // 2
        self.dp = lax.axis_index("dp")
        self.mp = lax.axis_index("mp")
        self.me = self.dp * mp_size + self.mp
        self.z = self.dp // 2
        self.y = lax.rem(self.dp, 2)
        self.x = self.mp // 2
        self.core = lax.rem(self.mp, 2)

    def at(self, linear):
        return (linear // self.mp_size, lax.rem(linear, self.mp_size))

    def next(self, step):
        return self.at(lax.rem(self.me + self.count + step, self.count))

    def core_peer(self):
        return (self.dp, self.mp + 1 - 2 * self.core)

    def x_peer(self):
        return (self.dp, self.mp + 2 - 4 * self.x)

    def y_peer(self):
        return (self.dp + 1 - 2 * self.y, self.mp)

    def z_peer(self, step):
        return (lax.rem(self.z + step, self.high) * 2 + self.y, self.mp)

    def greet_all(self):
        barrier = pltpu.get_barrier_semaphore()

        def greet_one(k):
            pl.semaphore_signal(barrier, inc=1, device_id=self.next(k + 1), device_id_type=MESH)

        loop(self.count - 1, greet_one)
        pl.semaphore_wait(barrier, self.count - 1)


def remote(src, dst, send, recv, peer):
    return pltpu.make_async_remote_copy(
        src_ref=src,
        dst_ref=dst,
        send_sem=send,
        recv_sem=recv,
        device_id=peer,
        device_id_type=MESH,
    )


def slab(index, size):
    return pl.ds(pl.multiple_of(index * size, size), size)


def loop(count, body):
    def step(i, carry):
        body(i)
        return carry

    lax.fori_loop(0, count, step, 0)


def launch(kernel, ins, specs, outs, out_specs, scratch, collective_id, vmem_mib):
    flat_in, tree_in = jax.tree.flatten(ins)
    flat_out, tree_out = jax.tree.flatten(outs)
    is_leaf = lambda s: not isinstance(s, (dict, list))
    flat_scratch, tree_scratch = jax.tree.flatten(scratch, is_leaf=is_leaf)
    spec_in = [s for n in sorted(ins) for s in [specs.get(n, vmem)] * len(jax.tree.leaves(ins[n]))]
    spec_out = [
        s for n in sorted(outs) for s in [out_specs.get(n, anywhere)] * len(jax.tree.leaves(outs[n]))
    ]

    def body(*refs):
        a, b = len(flat_in), len(flat_in) + len(flat_out)
        everything = dict(jax.tree.unflatten(tree_in, refs[:a]))
        everything.update(jax.tree.unflatten(tree_out, refs[a:b]))
        everything.update(jax.tree.unflatten(tree_scratch, refs[b:]))
        kernel(SimpleNamespace(**everything))

    results = pl.pallas_call(
        body,
        out_shape=flat_out,
        in_specs=spec_in,
        out_specs=spec_out,
        scratch_shapes=flat_scratch,
        compiler_params=pltpu.CompilerParams(
            collective_id=collective_id,
            has_side_effects=True,
            vmem_limit_bytes=vmem_mib * 1024 * 1024,
        ),
        name=kernel.func.__name__,
    )(*flat_in)
    return SimpleNamespace(**jax.tree.unflatten(tree_out, results))


def gelu_of(v):
    return 0.5 * v * (1.0 + jnp.tanh(v * (gelu_a + gelu_b * v * v)))


def gelu_slope(v):
    square = v * v
    t = jnp.tanh(v * (gelu_a + gelu_b * square))
    return 0.5 * (1.0 + t) + 0.5 * v * (1.0 - t * t) * (gelu_a + 3.0 * gelu_b * square)


def wide_valid(valid, rows, width):
    mask = valid[rows, :]
    return jnp.concatenate([mask] * (width // 128), axis=1)


def fold8(x):
    return jnp.sum(x.reshape(x.shape[0] // 8, 8, x.shape[1]), axis=0)


def strip_sums(pixel_count, width, terms, out, row_at):
    for block in range(width // lane_block):
        lanes = pl.ds(block * lane_block, lane_block)

        def step(i, carry, lanes=lanes):
            parts = terms(slab(i, strip), lanes)
            return tuple(c + fold8(p) for c, p in zip(carry, parts))

        zeros = tuple(jnp.zeros((8, lane_block), f32) for _ in row_at)
        sums = lax.fori_loop(0, pixel_count // strip, step, zeros)
        for row, total in zip(row_at, sums):
            out[row : row + 1, lanes] = jnp.sum(total, axis=0, keepdims=True)


def merge(parts, moments_mode):
    if not moments_mode:
        return jnp.sum(parts, axis=0)
    pixels, sums, squares = parts[:, 0:1], parts[:, 1:2], parts[:, 2:3]
    all_pixels, all_sums = jnp.sum(pixels, axis=0), jnp.sum(sums, axis=0)
    apart = sums / pixels - (all_sums / all_pixels)[None]
    all_squares = jnp.sum(squares + pixels * apart * apart, axis=0)
    return jnp.concatenate([all_pixels, all_sums, all_squares], axis=0)


def sync_groups(width, sizes):
    count = sizes[0] * sizes[1]
    if count > 64:
        return (16, count // 16)
    return sizes[::-1] if width > 1024 else (count,)


def sync_scratch(plan, sizes):
    out = []
    for rows, width in plan:
        for size in sync_groups(width, sizes):
            out += [pltpu.VMEM((rows, width), f32), pltpu.VMEM((size, rows, width), f32), dma, dma]
    return out


class Syncs:
    def __init__(self, place, buffers):
        self.place, self.buffers = place, buffers
        self.at = 0

    def take(self, width):
        stages = []
        stride = 1
        for size in sync_groups(width, (self.place.dp_size, self.place.mp_size)):
            digit = lax.rem(self.place.me // stride, size)
            stages.append((stride, size, digit, self.buffers[self.at : self.at + 4]))
            self.at += 4
            stride *= size
        return stages

    def start(self, stage, value=None):
        stride, size, digit, (src, slots, send, recv) = stage
        me = self.place.me
        if value is not None:
            src[...] = value

        def push(k):
            peer = me + (lax.rem(digit + k + 1, size) - digit) * stride
            remote(src, slots.at[digit], send, recv, self.place.at(peer)).start()

        loop(size - 1, push)
        pltpu.make_async_copy(src, slots.at[digit], recv).start()

    def finish(self, stage, moments_mode):
        stride, size, digit, (src, slots, send, recv) = stage
        pltpu.make_async_copy(slots, slots, recv).wait()
        rest = slots.at[pl.ds(0, size - 1)]
        pltpu.make_async_copy(rest, rest, send).wait()
        return merge(slots[...], moments_mode)

    def rest(self, stages, moments_mode):
        value = self.finish(stages[0], moments_mode)
        for stage in stages[1:]:
            self.start(stage, value)
            value = self.finish(stage, moments_mode)
        return value


def shifted(x, shift):
    if shift == 0:
        return x
    pixels = x.shape[0]
    column = lax.broadcasted_iota(jnp.int32, x.shape, 0) % breadth + shift
    inside = (column >= 0) & (column < breadth)
    return jnp.where(inside, pltpu.roll(x, (-shift) % pixels, 0), 0.0)


def row_scales(masks, first_row, which, width):
    row_of = lax.broadcasted_iota(jnp.int32, (chunk, width), 0) // breadth
    scale = jnp.zeros((chunk, width), f32)
    for k in range(chunk // breadth):
        scale = jnp.where(row_of == k, masks[first_row + k, which], scale)
    return scale


def masked_rows(part, masks, first_row, which):
    scaled = []
    for k in range(part.shape[0] // breadth):
        piece = part[breadth * k : breadth * (k + 1)].astype(f32)
        scaled.append((piece * masks[first_row + k, which]).astype(bf16))
    return jnp.concatenate(scaled, axis=0)


def tap_terms(off, masks, row, tap_row, tap_col):
    lane = lax.broadcasted_iota(jnp.int32, (breadth, 2 * breadth), 1)
    sub = lax.broadcasted_iota(jnp.int32, (breadth, 2 * breadth), 0)
    upper = lane >= breadth
    apart = jnp.where(upper, lane - breadth, lane) - sub
    tap, shift = 3 * tap_row + tap_col, 2 * tap_col - 2
    oy, ox = off[:, 2 * tap : 2 * tap + 1], off[:, 2 * tap + 1 : 2 * tap + 2]
    low, high = masks[row, 2 * tap_row], masks[row, 2 * tap_row + 1]
    down = jnp.where(upper, oy * high, (1.0 - oy) * low)
    across = jnp.where(apart == shift, 1.0 - ox, jnp.where(apart == shift + 1, ox, 0.0))
    down_slope = jnp.where(upper, high, -low)
    across_slope = jnp.where(apart == shift, -1.0, jnp.where(apart == shift + 1, 1.0, 0.0))
    return down, across, down_slope, across_slope


def nt_dot(a, b):
    return lax.dot_general(a, b, (((1,), (1,)), ((), ())), preferred_element_type=f32)


def tn_dot(a, b):
    return lax.dot_general(a, b, (((0,), (0,)), ((), ())), preferred_element_type=f32)


def nn_dot(a, b):
    return jnp.dot(a, b, preferred_element_type=f32)


class Outbox:
    def __init__(self, sems):
        self.sems, self.running = sems, {}

    def put(self, at, src, dst):
        copy = pltpu.make_async_copy(src, dst, self.sems.at[at])
        copy.start()
        self.running[at] = copy

    def settle(self, *which):
        for at in which or list(self.running):
            self.running.pop(at).wait()


def load_weight(full, dst, sem):
    if len(full.shape) == 2:
        copy = pltpu.make_async_copy(full, dst, sem)
        copy.start()
        return copy
    block = full.shape[2]
    for z in range(full.shape[0]):
        for y in range(2):
            rows = pl.ds((2 * z + y) * block, block)
            pltpu.make_async_copy(full.at[z, y], dst.at[rows], sem).start()
    return pltpu.make_async_copy(dst, dst, sem)


class Gather:
    def __init__(self, place, r):
        self.place, self.fulls, self.sems = place, r.fulls, (r.gather_local, r.gather_send, r.gather_recv)
        self.shards = r.shards
        self.stage = [0] * 6
        self.running = [[] for _ in range(6)]

    def cols(self, array, x_at, core_at):
        width = self.shards[array].shape[1]
        return pl.ds(pl.multiple_of((2 * x_at + core_at) * width, 128), width)

    def copies(self, array, stage):
        place, full = self.place, self.fulls[array]
        high, z, y, x, core = place.high, place.z, place.y, place.x, place.core
        half = high // 2
        mine = self.cols(array, x, core)
        lower, upper = pl.ds(0, half), pl.ds(half, high - half)
        local, send, recv = self.sems
        if stage == 0:
            target = full.at[z, y, :, mine]
            own = pltpu.make_async_copy(self.shards[array], target, local.at[array])
            return [own] + [
                remote(
                    self.shards[array],
                    target,
                    send.at[array, k - 1],
                    recv.at[array, k - 1],
                    place.z_peer(k),
                )
                for k in range(1, high)
            ]
        if stage == 1:
            pairs = [
                (full.at[lower, y, :, mine], place.x_peer()),
                (full.at[upper, y, :, mine], place.y_peer()),
            ]
        elif stage == 2:
            pairs = [
                (full.at[lower, y, :, self.cols(array, 0, core)], place.y_peer()),
                (full.at[lower, y, :, self.cols(array, 1, core)], place.y_peer()),
                (full.at[upper, :, :, mine], place.x_peer()),
            ]
        else:
            pairs = [
                (full.at[:, :, :, self.cols(array, 0, core)], place.core_peer()),
                (full.at[:, :, :, self.cols(array, 1, core)], place.core_peer()),
            ]
        base = high - 1 + [0, 0, 2, 5][stage]
        return [
            remote(ref, ref, send.at[array, base + i], recv.at[array, base + i], peer)
            for i, (ref, peer) in enumerate(pairs)
        ]

    def advance(self, *arrays):
        for array in arrays if self.shards else ():
            for copy in self.running[array]:
                copy.wait()
            self.running[array] = []
            if self.stage[array] < 4:
                self.running[array] = self.copies(array, self.stage[array])
                for copy in self.running[array]:
                    copy.start()
            self.stage[array] += 1


def forward_pass(sizes, r):
    place = Place(*sizes)
    syncs = Syncs(place, r.syncs)
    gather = Gather(place, r)
    out = Outbox(r.out_sem)
    valid, masks, counts = r.valid, r.masks, r.counts
    first, third, ext, hidden = r.first, r.third, r.ext, r.hidden
    pixels, width, wide = first.shape[0], first.shape[1], third.shape[1]
    halo = halo_rows * breadth
    chunks = pixels // chunk

    def load(array, dst, sem):
        return load_weight(r.fulls[array], dst, r.load_sem.at[sem])

    def moments(ref, rstd, mean, during=()):
        block_width = ref.shape[1]
        stages = syncs.take(block_width)
        src = stages[0][3][0]

        def sums(at, lanes):
            return (ref[at, lanes] * wide_valid(valid, at, lane_block),)

        strip_sums(pixels, block_width, sums, src, [1])
        src[0:1, :] = jnp.full((1, block_width), counts[0], f32)

        def squares(at, lanes):
            centred = ref[at, lanes] - src[1:2, lanes] * counts[1]
            return (centred * centred * wide_valid(valid, at, lane_block),)

        strip_sums(pixels, block_width, squares, src, [2])
        syncs.start(stages[0])
        for call in during:
            call()
        merged = syncs.rest(stages, True)
        mean[...] = merged[1:2] / merged[0:1]
        rstd[...] = lax.rsqrt(merged[2:3] / merged[0:1] + norm_eps)

    def activate(norm, hat, target, target_row):
        mean, rstd = r.mean_narrow, r.rstd_narrow.at[norm : norm + 1, :]
        gain, bias = r.mid_gain.at[norm : norm + 1, :], r.mid_bias.at[norm : norm + 1, :]

        def body(i):
            at = slab(i, strip)
            normed = (first[at, :] - mean[...]) * rstd[...]
            hat[at, :] = normed.astype(bf16)
            act = gelu_of(normed * gain[...] + bias[...]) * wide_valid(valid, at, width)
            rows = pl.ds(pl.multiple_of(target_row + i * strip, strip), strip)
            target[rows, :] = act.astype(bf16)

        loop(pixels // strip, body)

    def narrow_moments(norm, during=()):
        moments(first, r.rstd_narrow.at[norm : norm + 1, :], r.mean_narrow, during)

    def project(lhs, weight, target):
        def body(i):
            at = slab(i, chunk)
            target[at, :] = nn_dot(lhs[at, :], weight[...])

        loop(chunks, body)

    def halo_copies(block):
        field = ext.at[block]
        send, recv = r.halo_send.at[block], r.halo_recv.at[block]
        return [
            remote(
                field.at[pl.ds(pixels, halo)],
                field.at[pl.ds(0, halo)],
                send.at[0],
                recv.at[0],
                place.next(1),
            ),
            remote(
                field.at[pl.ds(halo, halo)],
                field.at[pl.ds(pixels + halo, halo)],
                send.at[1],
                recv.at[1],
                place.next(-1),
            ),
        ]

    def mid_deformable(i, slot):
        field = ext.at[0]
        base = halo + i * chunk
        first_row = i * (chunk // breadth)
        total = jnp.zeros((chunk, 128), f32)
        for tap_row in range(3):
            start = pl.multiple_of(base + (2 * tap_row - 2) * breadth, breadth)
            part = nn_dot(field[pl.ds(start, chunk), :], r.offset_weight[tap_row])
            total = total + part * row_scales(masks, first_row, 2 * tap_row, 128)
        left = shifted(total, -2)
        middle = pltpu.roll(total, 128 - 32, 1)
        right = pltpu.roll(shifted(total, 2), 128 - 64, 1)
        lane = lax.broadcasted_iota(jnp.int32, total.shape, 1)
        raw = jnp.where(lane < 32, left + middle + right, 0.0) + r.offset_bias[...]
        tanh_raw = jnp.tanh(raw)
        r.tanh_raw[slab(i, chunk), :] = tanh_raw
        r.off[...] = 0.5 + 0.45 * tanh_raw

        def one_row(k):
            off = r.off[slab(k, breadth), :]
            for tap_row in range(3):
                weights = []
                for tap_col in range(3):
                    down, across, _, _ = tap_terms(off, masks, first_row + k, tap_row, tap_col)
                    weights.append((down * across).astype(bf16))
                start = pl.multiple_of(base + (k + 2 * tap_row - 2) * breadth, breadth)
                got = nn_dot(jnp.concatenate(weights, axis=0), field[pl.ds(start, 2 * breadth), :])
                for tap_col in range(3):
                    lanes = pl.ds((3 * tap_row + tap_col) * width, width)
                    piece = got[breadth * tap_col : breadth * (tap_col + 1)]
                    r.samp[slot, slab(k, breadth), lanes] = piece.astype(bf16)

        loop(chunk // breadth, one_row)
        first[slab(i, chunk), :] = nn_dot(r.samp[slot], r.w_mid[...])

    def mid_plain(i):
        field = ext.at[1]
        lhs = []
        for tap_row in range(3):
            start = pl.multiple_of(halo + i * chunk + (2 * tap_row - 2) * breadth, breadth)
            part = field[pl.ds(start, chunk), :]
            if tap_row != 1:
                part = masked_rows(part, masks, i * (chunk // breadth), 2 * tap_row)
            lhs.append(part)
        total = None
        for tap_col in range(3):
            partial_sum = None
            for tap_row in range(3):
                weight = r.w_mid[pl.ds((3 * tap_row + tap_col) * width, width), :]
                part = nn_dot(lhs[tap_row], weight)
                partial_sum = part if partial_sum is None else partial_sum + part
            partial_sum = shifted(partial_sum, 2 * tap_col - 2)
            total = partial_sum if total is None else total + partial_sum
        first[slab(i, chunk), :] = total

    def finish_block(block, inputs, result):
        gain, bias = r.out_gain.at[block : block + 1, :], r.out_bias.at[block : block + 1, :]
        mean, rstd = r.mean_wide, r.rstd_wide.at[block : block + 1, :]

        def body(i):
            at = slab(i, strip)
            mask = wide_valid(valid, at, lane_block)
            for j in range(wide // lane_block):
                lanes = pl.ds(j * lane_block, lane_block)
                normed = (third[at, lanes] - mean[:, lanes]) * rstd[:, lanes]
                r.hat3[at, lanes] = normed.astype(bf16)
                pre = inputs[at, lanes].astype(f32) + (normed * gain[:, lanes] + bias[:, lanes])
                result[at, lanes] = (mask * gelu_of(pre)).astype(bf16)

        loop(pixels // strip, body)

    def wide_moments(block, during=()):
        moments(third, r.rstd_wide.at[block : block + 1, :], r.mean_wide, during)

    def samp_copy(i):
        slot = i % 2
        return pltpu.make_async_copy(
            r.samp.at[slot], r.samp_out.at[slab(i, chunk)], r.samp_sem.at[slot]
        )

    place.greet_all()
    gather.advance(0)
    gather.advance(0, 1)
    gather.advance(0)
    gather.advance(0, 1, 2)
    gather.advance(0)
    load(0, r.w_in, 0).wait()
    project(r.image, r.w_in, first)
    gather.advance(1)
    narrow_moments(0, [lambda: gather.advance(2)])
    gather.advance(3)
    activate(0, r.hat_a, ext.at[0], halo)
    out.put(0, r.hat_a, r.hat1_out[0])
    edges = halo_copies(0)
    for copy in edges:
        copy.start()
    gather.advance(1, 2, 3)
    for copy in edges:
        copy.wait()
    out.put(1, ext.at[0], r.field_out[0])
    gather.advance(1)
    gather.advance(4)
    load(1, r.w_mid, 1).wait()
    for i in range(chunks):
        if i >= 2:
            samp_copy(i - 2).wait()
        mid_deformable(i, i % 2)
        samp_copy(i).start()
        gather.advance(*{0: (2, 3), 1: (2, 3), 2: (3, 4, 5)}.get(i, ()))
    loaded = load(2, r.w_out, 2)
    loaded_in = load(3, r.w_in, 0)
    narrow_moments(1, [lambda: gather.advance(4, 5)])
    activate(1, r.hat_b, hidden, 0)
    out.put(2, r.hat_b, r.hat2_out[0])
    out.put(3, hidden, r.hidden_out[0])
    loaded.wait()
    project(hidden, r.w_out, third)
    wide_moments(0, [lambda: gather.advance(4, 5)])
    finish_block(0, r.image, r.middle)
    out.put(4, r.middle, r.middle_out)
    out.put(5, r.hat3, r.hat3_out[0])
    loaded_in.wait()
    gather.advance(4, 5)
    project(r.middle, r.w_in, first)
    gather.advance(4)
    loaded = load(4, r.w_mid, 1)
    narrow_moments(2, [lambda: gather.advance(5)])
    out.settle(0)
    activate(2, r.hat_a, ext.at[1], halo)
    out.put(0, r.hat_a, r.hat1_out[1])
    edges = halo_copies(1)
    for copy in edges:
        copy.start()
    loaded_out = load(5, r.w_out, 2)
    loaded.wait()
    for copy in edges:
        copy.wait()
    out.put(6, ext.at[1], r.field_out[1])
    loop(chunks, mid_plain)
    narrow_moments(3)
    out.settle(2, 3)
    activate(3, r.hat_b, hidden, 0)
    out.put(2, r.hat_b, r.hat2_out[1])
    out.put(3, hidden, r.hidden_out[1])
    loaded_out.wait()
    project(hidden, r.w_out, third)
    wide_moments(1)
    out.settle(5)
    finish_block(1, r.middle, r.result)
    out.put(7, r.result, r.image_out)
    out.put(5, r.hat3, r.hat3_out[1])
    for i in range(max(0, chunks - 2), chunks):
        samp_copy(i).wait()
    out.settle()


def forward(image, shards, geometry, offset_weight, offset_bias, mid_norms, out_norms, sizes):
    valid, masks, counts = geometry
    pixels, wide = image.shape
    width = shards[0].shape[1] * sizes[1]
    taps = 9 * width
    high = sizes[0] // 2
    ext_pixels = pixels + 2 * halo_rows * breadth
    in_kernel = all(s.shape[0] % 16 == 0 for s in shards)
    fulls = []
    if not in_kernel:
        fulls = [lax.all_gather(s, "mp", axis=1, tiled=True) for s in shards]
        fulls = [lax.all_gather(s, "dp", axis=0, tiled=True) for s in fulls]
    ins = dict(
        image=image,
        valid=valid,
        masks=masks,
        counts=counts,
        offset_weight=offset_weight,
        offset_bias=offset_bias,
        mid_gain=mid_norms[0],
        mid_bias=mid_norms[1],
        out_gain=out_norms[0],
        out_bias=out_norms[1],
        shards=list(shards) if in_kernel else [],
    )
    narrow, broad = shape((pixels, width), bf16), shape((pixels, wide), bf16)
    outs = dict(
        hat1_out=[narrow] * 2,
        hat2_out=[narrow] * 2,
        hidden_out=[narrow] * 2,
        field_out=[shape((ext_pixels, width), bf16)] * 2,
        hat3_out=[broad] * 2,
        middle_out=broad,
        image_out=broad,
        samp_out=shape((pixels, taps), bf16),
        tanh_raw=shape((pixels, 128), f32),
        rstd_narrow=shape((4, width), f32),
        rstd_wide=shape((2, wide), f32),
    )
    if in_kernel:
        outs.update(
            fulls=[shape((high, 2, s.shape[0], s.shape[1] * sizes[1]), bf16) for s in shards]
        )
    else:
        ins.update(fulls=fulls)
    plan = [(3, width), (3, width), (3, wide)] * 2
    scratch = dict(
        first=pltpu.VMEM((pixels, width), f32),
        third=pltpu.VMEM((pixels, wide), f32),
        ext=pltpu.VMEM((2, ext_pixels, width), bf16),
        hidden=pltpu.VMEM((pixels, width), bf16),
        hat_a=pltpu.VMEM((pixels, width), bf16),
        hat_b=pltpu.VMEM((pixels, width), bf16),
        hat3=pltpu.VMEM((pixels, wide), bf16),
        middle=pltpu.VMEM((pixels, wide), bf16),
        result=pltpu.VMEM((pixels, wide), bf16),
        samp=pltpu.VMEM((2, chunk, taps), bf16),
        off=pltpu.VMEM((chunk, 128), f32),
        w_in=pltpu.VMEM((wide, width), bf16),
        w_mid=pltpu.VMEM((taps, width), bf16),
        w_out=pltpu.VMEM((width, wide), bf16),
        mean_narrow=pltpu.VMEM((1, width), f32),
        mean_wide=pltpu.VMEM((1, wide), f32),
        gather_local=dma((6,)),
        gather_send=dma((6, high - 1 + 7)),
        gather_recv=dma((6, high - 1 + 7)),
        halo_send=dma((2, 2)),
        halo_recv=dma((2, 2)),
        out_sem=dma((8,)),
        samp_sem=dma((2,)),
        load_sem=dma((3,)),
        syncs=sync_scratch(plan, sizes),
    )
    kept = launch(
        partial(forward_pass, sizes),
        ins,
        dict(shards=anywhere, fulls=anywhere, masks=smem, counts=smem),
        outs,
        dict(tanh_raw=vmem, rstd_narrow=vmem, rstd_wide=vmem),
        scratch,
        0,
        62,
    )
    if not in_kernel:
        kept.fulls = fulls
    return kept


class Scatter:
    def __init__(self, place, r, kind, use, result):
        self.place, self.use, self.result = place, use, result
        self.keep, self.from_core = r.keep[kind], r.from_core[kind]
        self.low, self.upper = r.from_low[kind], r.from_upper[kind]
        self.two, self.from_high = r.from_two[kind], r.from_high[kind]
        self.send, self.recv, self.free = r.scatter_send[kind], r.scatter_recv[kind], r.scatter_free[kind]
        self.staging, self.staging_sem = r.staging, r.staging_sem
        self.rows, self.width = self.keep.shape[1], self.keep.shape[2]
        self.block = self.rows // place.dp_size
        self.tiles = self.rows // lane_block
        self.stage = 0
        self.running = []

    def cols(self, x_at, core_at):
        return pl.ds(pl.multiple_of((2 * x_at + core_at) * self.width, 128), self.width)

    def at(self, high, y):
        return pl.ds(pl.multiple_of((2 * high + y) * self.block, self.block), self.block)

    def to_core(self, t, i, src):
        rows = pl.ds(pl.multiple_of(t * lane_block, lane_block), lane_block)
        return remote(
            src,
            self.from_core.at[i, rows],
            self.send.at[2 * t + i],
            self.recv.at[2 * t + i],
            self.place.core_peer(),
        )

    def tile_copies(self, t):
        slot = lax.rem(t, 2)
        rows = pl.ds(pl.multiple_of(t * lane_block, lane_block), lane_block)
        core = self.place.core
        away = [self.to_core(t, i, self.staging.at[slot, :, self.cols(i, 1 - core)]) for i in (0, 1)]
        home = [
            pltpu.make_async_copy(
                self.staging.at[slot, :, self.cols(i, core)],
                self.keep.at[i, rows],
                self.staging_sem.at[slot, i],
            )
            for i in (0, 1)
        ]
        return away, home

    def settle_tile(self, t):
        away, home = self.tile_copies(t)
        for copy in away:
            copy.wait_send()
        for copy in home:
            copy.wait()

    def begin(self):
        if self.use == 1:
            pl.semaphore_wait(self.free.at[0], 1)

    def fill(self, first, last, compute):
        def body(i):
            t = first + i

            @pl.when(i >= 2)
            def _():
                self.settle_tile(t - 2)

            compute(t, self.staging.at[lax.rem(t, 2)])
            away, home = self.tile_copies(t)
            for copy in away + home:
                copy.start()

        loop(last - first, body)
        for t in range(max(first, last - 2), last):
            self.settle_tile(t)

    def fill_by_columns(self, compute):
        core = self.place.core

        def away(i):
            self.staging[i] = compute(self.cols(i, 1 - core)).astype(bf16)
            self.to_core(0, i, self.staging.at[i]).start()

        def home(i):
            self.keep[i] = compute(self.cols(i, core)).astype(bf16)

        loop(2, away)
        loop(2, home)
        for i in (0, 1):
            self.to_core(0, i, self.staging.at[i]).wait_send()

    def copies(self, stage):
        place = self.place
        x, y, z, half = place.x, place.y, place.z, place.high // 2
        items = []
        if stage == 1:
            for i in (0, 1):
                for b in range(half):
                    items.append((self.keep.at[i, self.at(b, 1 - y)], self.low.at[i, b], place.y_peer()))
            upper = pl.ds(self.rows // 2, self.rows // 2)
            items.append((self.keep.at[1 - x, upper], self.upper, place.x_peer()))
        elif stage == 2:
            for b in range(half):
                items.append((self.keep.at[1 - x, self.at(b, y)], self.two.at[0, b], place.x_peer()))
                items.append(
                    (self.keep.at[x, self.at(half + b, 1 - y)], self.two.at[1, b], place.y_peer())
                )
        else:
            for k in range(1, place.high):
                there = self.at(lax.rem(z + k, place.high), y)
                items.append((self.keep.at[x, there], self.from_high.at[k - 1], place.z_peer(k)))
        base = 2 * self.tiles + [0, 0, 2 * half + 1, 4 * half + 1][stage]
        return [
            remote(src, dst, self.send.at[base + i], self.recv.at[base + i], peer)
            for i, (src, dst, peer) in enumerate(items)
        ]

    def add(self, target, extra):
        target[...] = (target[...].astype(f32) + extra[...].astype(f32)).astype(bf16)

    def finish(self, stage):
        place = self.place
        x, y, z, half = place.x, place.y, place.z, place.high // 2
        if stage == 0:
            piece = 64
            for i in (0, 1):

                def body(k, i=i):
                    rows = slab(k, piece)
                    self.add(self.keep.at[i, rows], self.from_core.at[i, rows])

                loop(self.rows // piece, body)
            peers = [place.core_peer()]
        elif stage == 1:
            for b in range(half):
                for i in (0, 1):
                    self.add(self.keep.at[i, self.at(b, y)], self.low.at[i, b])
            piece = 64

            def body(k):
                rows = pl.ds(pl.multiple_of(self.rows // 2 + k * piece, piece), piece)
                self.add(self.keep.at[x, rows], self.upper.at[slab(k, piece)])

            loop(self.rows // 2 // piece, body)
            peers = [place.x_peer(), place.y_peer()]
        elif stage == 2:
            for b in range(half):
                self.add(self.keep.at[x, self.at(b, y)], self.two.at[0, b])
                self.add(self.keep.at[x, self.at(half + b, y)], self.two.at[1, b])
            peers = [place.x_peer(), place.y_peer()]
        else:
            total = self.keep[x, self.at(z, y)].astype(f32)
            for k in range(1, place.high):
                total = total + self.from_high[k - 1].astype(f32)
            self.result[...] = total
            peers = [place.z_peer(k) for k in range(1, place.high)]
        if self.use == 0:
            for peer in peers:
                pl.semaphore_signal(self.free.at[stage], inc=1, device_id=peer, device_id_type=MESH)

    def advance(self):
        if self.stage > 3:
            return
        if self.stage == 0:
            for t in range(self.tiles):
                for i in (0, 1):
                    self.to_core(t, i, self.staging.at[0, :, self.cols(i, 0)] if self.tiles > 1 else self.staging.at[i]).wait_recv()
        for copy in self.running:
            copy.wait()
        self.finish(self.stage)
        self.stage += 1
        if self.stage <= 3:
            if self.use == 1:
                waits = [0, 2, 2, self.place.high - 1][self.stage]
                pl.semaphore_wait(self.free.at[self.stage], waits)
            self.running = self.copies(self.stage)
            for copy in self.running:
                copy.start()

    def drain(self):
        while self.stage <= 3:
            self.advance()


class Whole:
    def __init__(self, r, result):
        self.staging, self.staging_sem, self.result = r.staging, r.staging_sem, result

    def begin(self):
        pass

    def fill(self, first, last, compute):
        def body(i):
            t = first + i
            compute(t, self.staging.at[0])
            rows = pl.ds(pl.multiple_of(t * lane_block, lane_block), lane_block)
            pltpu.sync_copy(self.staging.at[0], self.result.at[rows])

        loop(last - first, body)

    def fill_by_columns(self, compute):
        def body(i):
            lanes = pl.ds(pl.multiple_of(i * lane_block, lane_block), lane_block)
            self.staging[0] = compute(lanes).astype(bf16)
            pltpu.sync_copy(self.staging.at[0], self.result.at[:, lanes])

        loop(self.result.shape[1] // lane_block, body)

    def advance(self):
        pass

    drain = advance


def backward_pass(sizes, in_kernel, r):
    place = Place(*sizes)
    syncs = Syncs(place, r.syncs)
    box = Outbox(r.load_sem)
    valid, masks, counts = r.valid, r.masks, r.counts
    grad, small, inputs, hat3, wide_act = r.grad, r.small, r.inputs, r.hat3, r.wide_act
    pixels, wide, width = grad.shape[0], grad.shape[1], small.shape[1]
    halo = halo_rows * breadth
    chunks, chunk_rows = pixels // chunk, chunk // breadth
    per_pixel = counts[2]
    own = pl.ds(halo, pixels)
    kinds = [0, 1, 2]

    def scatter(kind, use):
        result = r.grads[3 * use + kind]
        if in_kernel:
            return Scatter(place, r, kind, use, result)
        return Whole(r, result)

    def weight(array, dst, sem):
        box.running[sem] = load_weight(r.fulls[array], dst, r.load_sem.at[sem])

    def open_sync(terms, block_width, rows=2, last_row=None):
        stages = syncs.take(block_width)
        src = stages[0][3][0]
        strip_sums(pixels, block_width, terms, src, [0, 1])
        if last_row is not None:
            src[2:3, :] = jnp.zeros((1, block_width), f32)
            src[2:3, 0:128] = last_row
        syncs.start(stages[0])
        return stages

    def pre_back(block, upstream, image):
        gain, bias = r.out_gain.at[block : block + 1, :], r.out_bias.at[block : block + 1, :]

        def terms(at, lanes):
            hat = hat3[at, lanes].astype(f32)
            pre = image[at, lanes].astype(f32) + (hat * gain[:, lanes] + bias[:, lanes])
            slope = gelu_slope(pre) * wide_valid(valid, at, lane_block)
            d = upstream[at, lanes].astype(f32) * slope
            grad[at, lanes] = d
            return d, d * hat

        return open_sync(terms, wide)

    def last_norm_back(block):
        sums, rstd = r.wide_sums.at[block], r.rstd_wide.at[block : block + 1, :]
        gain = r.out_gain.at[block : block + 1, :]

        def body(i):
            at = slab(i, strip)
            mask = wide_valid(valid, at, lane_block)
            for j in range(wide // lane_block):
                lanes = pl.ds(j * lane_block, lane_block)
                hat = hat3[at, lanes].astype(f32)
                inner = grad[at, lanes] - sums[0:1, lanes] * per_pixel
                inner = inner - hat * (sums[1:2, lanes] * per_pixel)
                scaled = mask * (gain[:, lanes] * rstd[:, lanes]) * inner
                wide_act[at, lanes] = scaled.astype(bf16)

        loop(pixels // strip, body)

    def act_back(norm, hat):
        gain, bias = r.mid_gain.at[norm : norm + 1, :], r.mid_bias.at[norm : norm + 1, :]

        def terms(at, lanes):
            normed = hat[at, lanes].astype(f32)
            slope = gelu_slope(normed * gain[:, lanes] + bias[:, lanes])
            rows = pl.ds(pl.multiple_of(halo + at.start, strip), strip)
            d = small[rows, lanes] * slope * wide_valid(valid, at, lane_block)
            small[rows, lanes] = d
            return d, d * normed

        return terms

    def inner_norm_back(norm, hat, target, target_row):
        sums, rstd = r.narrow_sums.at[norm], r.rstd_narrow.at[norm : norm + 1, :]
        gain = r.mid_gain.at[norm : norm + 1, :]

        def body(i):
            at = slab(i, strip)
            rows = pl.ds(pl.multiple_of(halo + i * strip, strip), strip)
            inner = small[rows, :] - sums[0:1, :] * per_pixel
            inner = inner - hat[at, :].astype(f32) * (sums[1:2, :] * per_pixel)
            scaled = wide_valid(valid, at, width) * (gain[...] * rstd[...]) * inner
            target[pl.ds(pl.multiple_of(target_row + i * strip, strip), strip), :] = scaled.astype(bf16)

        loop(pixels // strip, body)

    def out_back(block):
        def body(i):
            rows = pl.ds(pl.multiple_of(halo + i * chunk, breadth), chunk)
            small[rows, :] = nt_dot(wide_act[slab(i, chunk), :], r.w_out[...])

        loop(chunks, body)
        return open_sync(act_back(2 * block + 1, r.hat2), width)

    def out_grad(target):
        target.begin()
        target.fill_by_columns(lambda lanes: tn_dot(r.hidden[...], wide_act[:, lanes]))

    def in_grad(target):
        target.begin()

        def compute(t, ref):
            lanes = pl.ds(pl.multiple_of(t * lane_block, lane_block), lane_block)
            ref[...] = tn_dot(inputs[:, lanes], r.da[...]).astype(bf16)

        target.fill(0, wide // lane_block, compute)

    def in_back(i):
        at = slab(i, chunk)
        grad[at, :] = grad[at, :] + nt_dot(r.da[at, :], r.w_in[...])

    def neighbours(before_src, before_dst, after_src, after_dst, which):
        send, recv = r.edge_send.at[which], r.edge_recv.at[which]
        return [
            remote(after_src, after_dst, send.at[0], recv.at[0], place.next(1)),
            remote(before_src, before_dst, send.at[1], recv.at[1], place.next(-1)),
        ]

    place.greet_all()
    box.put(0, r.middle, inputs)
    box.put(1, r.hat3_in[1], hat3)
    box.put(2, r.cotangent, wide_act)
    weight(5, r.w_out, 3)
    box.put(4, r.hat2_in[1], r.hat2)
    box.put(5, r.hidden_in[1], r.hidden)
    box.put(6, r.field_in[1].at[own], r.field.at[own])
    weight(4, r.w_mid, 7)
    weight(3, r.w_in, 8)

    out_b, mid_b, in_b = [scatter(kind, 0) for kind in kinds]
    box.settle(0, 1, 2)
    stages = pre_back(1, wide_act, inputs)
    r.wide_sums[1] = syncs.rest(stages, False)
    last_norm_back(1)
    box.put(1, r.hat3_in[0], hat3)
    box.settle(3, 4)
    stages = out_back(1)
    box.settle(5)
    out_grad(out_b)
    box.put(2, r.image, wide_act)
    weight(2, r.w_out, 3)
    r.narrow_sums[3] = syncs.rest(stages, False)
    box.put(5, r.hat1_in[1], r.hidden)

    pool, side = r.pool, 2 * breadth
    span = pixels + 2 * side
    centre = 2 * span
    inner_norm_back(3, r.hat2, pool, centre + side)
    box.put(4, r.hat2_in[0], r.hat2)
    edges = neighbours(
        pool.at[pl.ds(centre + side, side)],
        pool.at[pl.ds(centre + side + pixels, side)],
        pool.at[pl.ds(centre + pixels, side)],
        pool.at[pl.ds(centre, side)],
        0,
    )
    for copy in edges:
        copy.start()

    def shift_row(row):
        at = pl.ds(pl.multiple_of(centre + row * breadth, breadth), breadth)
        value = pool[at, :].astype(f32)
        for slot, amount in ((0, 2), (1, -2)):
            rows = pl.ds(pl.multiple_of(slot * span + row * breadth, breadth), breadth)
            pool[rows, :] = shifted(value, amount).astype(bf16)

    loop(pixels // breadth, lambda row: shift_row(row + 2))
    out_b.advance()
    for copy in edges:
        copy.wait()
    loop(2, shift_row)
    loop(2, lambda row: shift_row(row + 2 + pixels // breadth))
    slot_of = (0, 2, 1)
    box.settle(6, 7)

    def mid_back_plain(i):
        first_row = i * chunk_rows
        total = None
        for tap_row in range(3):
            for tap_col in range(3):
                start = slot_of[tap_col] * span + (4 - 2 * tap_row) * breadth + i * chunk
                part = pool[pl.ds(pl.multiple_of(start, breadth), chunk), :]
                if tap_row != 1:
                    part = masked_rows(part, masks, first_row, 4 - 2 * tap_row)
                tap = pl.ds((3 * tap_row + tap_col) * width, width)
                term = nt_dot(part, r.w_mid[tap, :])
                total = term if total is None else total + term
        rows = pl.ds(pl.multiple_of(halo + i * chunk, breadth), chunk)
        small[rows, :] = total

    loop(chunks, mid_back_plain)
    weight(1, r.w_mid, 7)
    out_b.advance()
    box.settle(5)
    stages = open_sync(act_back(2, r.hidden), width)
    mid_b.begin()
    shifted_rows = 3 * span

    def mid_grad_plain(t, ref):
        tap_row, tap_col = t // 3, lax.rem(t, 3)
        slot = jnp.where(tap_col == 0, 0, jnp.where(tap_col == 1, 2, 1))

        def copy_row(row):
            start = slot * span + (4 - 2 * tap_row + row) * breadth
            part = pool[pl.ds(pl.multiple_of(start, breadth), breadth), :]
            rows = pl.ds(pl.multiple_of(shifted_rows + row * breadth, breadth), breadth)
            pool[rows, :] = masked_rows(part, masks, row, 4 - 2 * tap_row)

        loop(pixels // breadth, copy_row)
        ref[...] = tn_dot(r.field[own, :], pool[pl.ds(shifted_rows, pixels), :]).astype(bf16)

    mid_b.fill(0, 9, mid_grad_plain)
    out_b.advance()
    r.narrow_sums[2] = syncs.rest(stages, False)
    inner_norm_back(2, r.hidden, r.da, 0)
    box.put(5, r.hidden_in[0], r.hidden)
    box.put(6, r.field_in[0], r.field)
    box.settle(8)
    loop(chunks, in_back)
    out_b.advance()
    mid_b.advance()
    weight(0, r.w_in, 8)

    out_a, mid_a, in_a = [scatter(kind, 1) for kind in kinds]
    box.settle(1, 2)
    stages = pre_back(0, grad, wide_act)
    in_grad(in_b)
    mid_b.advance()
    r.wide_sums[0] = syncs.rest(stages, False)
    box.put(0, r.image, inputs)
    last_norm_back(0)
    mid_b.advance()
    box.settle(3, 4)
    stages = out_back(0)
    box.settle(5)
    out_b.drain()
    out_grad(out_a)
    in_b.advance()
    mid_b.advance()
    r.narrow_sums[1] = syncs.rest(stages, False)
    inner_norm_back(1, r.hat2, r.da, 0)
    box.put(5, r.hat1_in[0], r.hidden)
    box.settle(6, 7)

    def clear(i):
        small[slab(i, breadth), :] = jnp.zeros((breadth, width), f32)

    loop((pixels + 2 * halo) // breadth, clear)
    table = r.table
    table[...] = jnp.zeros_like(table)
    r.draw_sum[...] = jnp.zeros_like(r.draw_sum)

    def mid_back_deformable(i):
        first_row = i * chunk_rows
        part = r.da[slab(i, chunk), :]
        for tap_row in range(3):
            for tap_col in range(3):
                tap = pl.ds((3 * tap_row + tap_col) * width, width)
                dsamp = nt_dot(part, r.w_mid[tap, :]).astype(bf16)
                for k in range(chunk_rows):
                    start = ((tap_row * chunk_rows + k) * 3 + tap_col) * breadth
                    pool[pl.ds(start, breadth), :] = dsamp[breadth * k : breadth * (k + 1)]
        th = r.tanh_raw[slab(i, chunk), :]
        r.off[...] = 0.5 + 0.45 * th
        lane = lax.broadcasted_iota(jnp.int32, (breadth, 128), 1)

        def one_row(k):
            off = r.off[slab(k, breadth), :]
            doff = jnp.zeros((breadth, 128), f32)
            for tap_row in range(3):
                start = (tap_row * chunk_rows + k) * 3 * breadth
                dsamp = pool[pl.ds(pl.multiple_of(start, breadth), 3 * breadth), :]
                start = halo + i * chunk + (k + 2 * tap_row - 2) * breadth
                rows = pl.ds(pl.multiple_of(start, breadth), 2 * breadth)
                dots = nt_dot(dsamp, r.field[rows, :])
                weights = []
                for tap_col in range(3):
                    terms = tap_terms(off, masks, first_row + k, tap_row, tap_col)
                    down, across, down_slope, across_slope = terms
                    weights.append((down * across).astype(bf16))
                    part = dots[breadth * tap_col : breadth * (tap_col + 1)]
                    doy = jnp.sum(part * (across * down_slope), axis=1, keepdims=True)
                    dox = jnp.sum(part * (across_slope * down), axis=1, keepdims=True)
                    tap = 3 * tap_row + tap_col
                    doff = jnp.where(lane == 2 * tap, doy, jnp.where(lane == 2 * tap + 1, dox, doff))
                small[rows, :] = small[rows, :] + tn_dot(jnp.concatenate(weights, axis=0), dsamp)
            th_row = r.tanh_raw[pl.ds(pl.multiple_of(i * chunk + k * breadth, breadth), breadth), :]
            draw = (0.45 * (1.0 - th_row * th_row) * doff).astype(bf16).astype(f32)
            r.off[slab(k, breadth), :] = draw
            r.draw_sum[...] = r.draw_sum[...] + fold8(draw)

        loop(chunk_rows, one_row)
        draw = r.off[...]
        spread = shifted(draw, 2) + pltpu.roll(draw, 32, 1) + pltpu.roll(shifted(draw, -2), 64, 1)
        for tap_row in range(3):
            part = (spread * row_scales(masks, first_row, 2 * tap_row, 128)).astype(bf16)
            start = halo + i * chunk + (2 * tap_row - 2) * breadth
            rows = pl.ds(pl.multiple_of(start, breadth), chunk)
            small[rows, :] = small[rows, :] + nt_dot(part, r.offset_weight[tap_row])
            to = pl.ds(tap_row * width, width)
            table[to, :] = table[to, :] + tn_dot(r.field[rows, :], part)

    def deform_part(first, last):
        loop(last - first, lambda i: mid_back_deformable(first + i))

    deform_part(0, chunks // 2)
    in_b.advance()
    mid_b.drain()
    out_a.advance()
    deform_part(chunks // 2, chunks)

    r.rims[0] = small[pl.ds(0, halo), :].astype(bf16)
    r.rims[1] = small[pl.ds(halo + pixels, halo), :].astype(bf16)
    edges = neighbours(r.rims.at[0], r.got_rims.at[0], r.rims.at[1], r.got_rims.at[1], 1)
    for copy in edges:
        copy.start()

    each = table.shape[0] // place.count

    def slice_of(device):
        return pl.ds(pl.multiple_of(device * each, each), each)

    def push(k):
        to = lax.rem(place.me + k + 1, place.count)
        remote(
            table.at[slice_of(to)], r.table_got.at[place.me], r.table_sem.at[0], r.table_sem.at[1], place.at(to)
        ).start()

    loop(place.count - 1, push)
    pltpu.make_async_copy(
        table.at[slice_of(place.me)], r.table_got.at[place.me], r.table_sem.at[1]
    ).start()

    mid_a.begin()
    slots = 9 * chunk

    def samp_load(t):
        slot = pl.ds(pl.multiple_of(slots + lax.rem(t, 2) * pixels, breadth), pixels)
        lanes = pl.ds(pl.multiple_of(t * width, 128), width)
        return pltpu.make_async_copy(r.samp_in.at[:, lanes], pool.at[slot], r.samp_sem.at[lax.rem(t, 2)])

    def mid_grad_deformable(t, ref):
        @pl.when(t < 8)
        def _():
            samp_load(t + 1).start()

        samp_load(t).wait()
        slot = pl.ds(pl.multiple_of(slots + lax.rem(t, 2) * pixels, breadth), pixels)
        ref[...] = tn_dot(pool[slot, :], r.da[...]).astype(bf16)

    samp_load(0).start()
    mid_a.fill(0, 4, mid_grad_deformable)
    in_b.advance()
    out_a.advance()
    for copy in edges:
        copy.wait()
    first_rows, last_rows = pl.ds(halo, halo), pl.ds(pixels, halo)
    small[first_rows, :] = small[first_rows, :] + r.got_rims[1].astype(f32)
    small[last_rows, :] = small[last_rows, :] + r.got_rims[0].astype(f32)
    box.settle(5)
    draw_sum = jnp.sum(r.draw_sum[...], axis=0, keepdims=True)
    stages = open_sync(act_back(0, r.hidden), width, 3, draw_sum)
    mid_a.fill(4, 9, mid_grad_deformable)
    in_b.advance()
    out_a.advance()

    got = r.table_got
    pltpu.make_async_copy(got, got, r.table_sem.at[1]).wait()
    rest = got.at[pl.ds(0, place.count - 1)]
    pltpu.make_async_copy(rest, rest, r.table_sem.at[0]).wait()
    r.table_total[...] = jnp.sum(got[...], axis=0)

    def push_total(k):
        remote(
            r.table_total,
            r.offset_grad.at[slice_of(place.me)],
            r.table_sem.at[2],
            r.table_sem.at[3],
            place.next(k + 1),
        ).start()

    loop(place.count - 1, push_total)
    pltpu.make_async_copy(
        r.table_total, r.offset_grad.at[slice_of(place.me)], r.table_sem.at[3]
    ).start()

    merged = syncs.rest(stages, False)
    r.narrow_sums[0] = merged[0:2]
    r.bias_sum[...] = merged[2:3, 0:128]
    inner_norm_back(0, r.hidden, r.da, 0)
    in_b.drain()
    mid_a.advance()
    box.settle(0)
    in_grad(in_a)
    out_a.drain()
    box.settle(8)
    for i in range(chunks):
        in_back(i)
        at = slab(i, chunk)
        box.put(9 + i, grad.at[at], r.image_grad.at[at])
        (mid_a if i % 2 else in_a).advance()
    in_a.drain()
    mid_a.drain()
    whole = r.offset_grad
    pltpu.make_async_copy(whole, whole, r.table_sem.at[3]).wait()
    rest = whole.at[pl.ds(0, (place.count - 1) * each)]
    pltpu.make_async_copy(rest, rest, r.table_sem.at[2]).wait()
    box.settle()


def backward(kept, image, cotangent, geometry, offset_weight, mid_norms, out_norms, sizes, in_kernel):
    valid, masks, counts = geometry
    pixels, wide = image.shape
    width = mid_norms[0].shape[1]
    taps = 9 * width
    count, high = sizes[0] * sizes[1], sizes[0] // 2
    half = high // 2
    ext_pixels = pixels + 2 * halo_rows * breadth
    each = 8 * (-(-3 * width // (8 * count)))
    fulls = [(width, wide), (taps, width), (wide, width)]
    owned = [(rows // sizes[0], cols // sizes[1]) for rows, cols in fulls]
    if in_kernel:
        grads = [shape(o, f32) for o in owned] * 2
        scatter = dict(
            keep=[pltpu.VMEM((2, rows, b), bf16) for (rows, _), (_, b) in zip(fulls, owned)],
            from_core=[pltpu.VMEM((2, rows, b), bf16) for (rows, _), (_, b) in zip(fulls, owned)],
            from_low=[pltpu.VMEM((2, half) + o, bf16) for o in owned],
            from_upper=[
                pltpu.VMEM((rows // 2, b), bf16) for (rows, _), (_, b) in zip(fulls, owned)
            ],
            from_two=[pltpu.VMEM((2, half) + o, bf16) for o in owned],
            from_high=[pltpu.VMEM((high - 1,) + o, bf16) for o in owned],
            scatter_free=[pltpu.SemaphoreType.REGULAR((4,))] * 3,
        )
        sems = [dma((2 * (rows // lane_block) + 4 * half + high,)) for rows, _ in fulls]
        scatter.update(scatter_send=sems, scatter_recv=sems)
    else:
        grads = [shape(full, bf16) for full in fulls] * 2
        scatter = dict()
    ins = dict(
        image=image,
        cotangent=cotangent,
        middle=kept.middle_out,
        hat1_in=kept.hat1_out,
        hat2_in=kept.hat2_out,
        hat3_in=kept.hat3_out,
        hidden_in=kept.hidden_out,
        field_in=kept.field_out,
        samp_in=kept.samp_out,
        fulls=kept.fulls,
        tanh_raw=kept.tanh_raw,
        rstd_narrow=kept.rstd_narrow,
        rstd_wide=kept.rstd_wide,
        valid=valid,
        masks=masks,
        counts=counts,
        offset_weight=offset_weight,
        mid_gain=mid_norms[0],
        mid_bias=mid_norms[1],
        out_gain=out_norms[0],
        out_bias=out_norms[1],
    )
    specs = dict(
        image=anywhere,
        cotangent=anywhere,
        middle=anywhere,
        hat1_in=anywhere,
        hat2_in=anywhere,
        hat3_in=anywhere,
        hidden_in=anywhere,
        field_in=anywhere,
        samp_in=anywhere,
        fulls=anywhere,
        masks=smem,
        counts=smem,
    )
    outs = dict(
        image_grad=shape((pixels, wide), f32),
        grads=grads,
        narrow_sums=shape((4, 2, width), f32),
        wide_sums=shape((2, 2, wide), f32),
        offset_grad=shape((count * each, 128), f32),
        bias_sum=shape((1, 128), f32),
    )
    out_specs = dict(narrow_sums=vmem, wide_sums=vmem, offset_grad=vmem, bias_sum=vmem)
    if in_kernel:
        out_specs.update(grads=vmem)
    plan = [(2, wide), (2, width), (2, width), (2, wide), (2, width), (3, width)]
    span = pixels + 4 * breadth
    pool_rows = max(3 * span + pixels, 9 * chunk + 2 * pixels)
    scratch = dict(
        grad=pltpu.VMEM((pixels, wide), f32),
        inputs=pltpu.VMEM((pixels, wide), bf16),
        hat3=pltpu.VMEM((pixels, wide), bf16),
        wide_act=pltpu.VMEM((pixels, wide), bf16),
        w_in=pltpu.VMEM((wide, width), bf16),
        w_mid=pltpu.VMEM((taps, width), bf16),
        w_out=pltpu.VMEM((width, wide), bf16),
        small=pltpu.VMEM((ext_pixels, width), f32),
        hat2=pltpu.VMEM((pixels, width), bf16),
        hidden=pltpu.VMEM((pixels, width), bf16),
        da=pltpu.VMEM((pixels, width), bf16),
        field=pltpu.VMEM((ext_pixels, width), bf16),
        pool=pltpu.VMEM((pool_rows, width), bf16),
        off=pltpu.VMEM((chunk, 128), f32),
        draw_sum=pltpu.VMEM((8, 128), f32),
        table=pltpu.VMEM((count * each, 128), f32),
        table_got=pltpu.VMEM((count, each, 128), f32),
        table_total=pltpu.VMEM((each, 128), f32),
        rims=pltpu.VMEM((2, halo_rows * breadth, width), bf16),
        got_rims=pltpu.VMEM((2, halo_rows * breadth, width), bf16),
        staging=pltpu.VMEM((2, lane_block, lane_block), bf16),
        staging_sem=dma((2, 2)),
        table_sem=dma((4,)),
        edge_send=dma((2, 2)),
        edge_recv=dma((2, 2)),
        samp_sem=dma((2,)),
        load_sem=dma((9 + pixels // chunk,)),
        syncs=sync_scratch(plan, sizes),
        **scatter,
    )
    return launch(
        partial(backward_pass, sizes, in_kernel), ins, specs, outs, out_specs, scratch, 1, 63
    )


def row_info(row_index, heights, widths, group_rows, total_rows):
    image_count = heights.shape[1]
    inside = (row_index >= 0) & (row_index < total_rows)
    group_of = jnp.clip(row_index // group_rows, 0, 1)
    local_row = row_index - group_of * group_rows
    image_ends = jnp.cumsum(heights, axis=1)
    is_first = (group_of == 0)[:, None]
    ends_by_row = jnp.where(is_first, image_ends[0][None, :], image_ends[1][None, :])
    image_num = jnp.sum((local_row[:, None] >= ends_by_row).astype(jnp.int32), axis=1)
    identity = jnp.where(inside, group_of * image_count + image_num, -1)
    width_table = jnp.where(is_first, widths[0][None, :], widths[1][None, :])
    picked = jnp.arange(image_count, dtype=jnp.int32)[None, :] == image_num[:, None]
    width_row = jnp.sum(jnp.where(picked, width_table, 0), axis=1)
    return (identity, jnp.where(inside, width_row, 0))


def per_device(
    image_in,
    cotangent,
    heights,
    widths,
    weight_in_a,
    weight_offset,
    bias_offset,
    weight_mid_a,
    weight_out_a,
    weight_in_b,
    weight_mid_b,
    weight_out_b,
    mid_gain,
    mid_bias,
    out_gain,
    out_bias,
):
    height, wide = image_in.shape[0], image_in.shape[2]
    sizes = (lax.axis_size("dp"), lax.axis_size("mp"))
    total_rows = height * sizes[0] * sizes[1]
    first_row = lax.axis_index(("dp", "mp")) * height
    row_index = first_row - halo_rows + jnp.arange(height + 2 * halo_rows, dtype=jnp.int32)
    identity, width_row = row_info(
        row_index, heights, widths, total_rows // 2 + height // 2, total_rows
    )
    centre = identity[halo_rows : halo_rows + height]
    masks = jnp.stack(
        [(identity[halo_rows + s : halo_rows + s + height] == centre) for s in range(-2, 4)], axis=1
    ).astype(f32)
    col_index = jnp.arange(breadth, dtype=jnp.int32)
    own_width = width_row[halo_rows : halo_rows + height]
    valid = (col_index[None, :] < own_width[:, None]).astype(f32)
    valid = jnp.broadcast_to(valid.reshape(-1, 1), (height * breadth, 128))
    local_pixels = jnp.sum(own_width).astype(f32)
    pixels = jnp.sum(heights * widths).astype(f32)
    counts = jnp.stack([local_pixels, 1.0 / local_pixels, 1.0 / pixels])
    geometry = (valid, masks, counts)
    width = weight_offset.shape[0] // 9
    by_tap = weight_offset.reshape(3, 3, width, offsets_count).transpose(0, 2, 1, 3)
    by_tap = jnp.pad(by_tap, ((0, 0), (0, 0), (0, 1), (0, 32 - offsets_count)))
    offset_weight = by_tap.reshape(3, width, 128)
    offset_bias = jnp.pad(bias_offset, (0, 128 - offsets_count))[None]
    mid_norms = (mid_gain.reshape(4, width), mid_bias.reshape(4, width))
    out_norms = (out_gain, out_bias)
    shards = (weight_in_a, weight_mid_a, weight_out_a, weight_in_b, weight_mid_b, weight_out_b)
    in_kernel = all(s.shape[0] % 16 == 0 for s in shards)
    image = image_in.reshape(height * breadth, wide)
    kept = forward(
        image, shards, geometry, offset_weight, offset_bias, mid_norms, out_norms, sizes
    )
    back = backward(
        kept,
        image,
        cotangent.reshape(height * breadth, wide),
        geometry,
        offset_weight,
        mid_norms,
        out_norms,
        sizes,
        in_kernel,
    )
    grads = back.grads
    if not in_kernel:
        grads = [
            lax.psum_scatter(
                lax.psum_scatter(g.astype(f32), "dp", scatter_dimension=0, tiled=True),
                "mp",
                scatter_dimension=1,
                tiled=True,
            )
            for g in grads
        ]
    offset_grad = back.offset_grad[: 3 * width].reshape(3, width, 4, 32)[:, :, :3, :offsets_count]
    offset_grad = offset_grad.transpose(0, 2, 1, 3).reshape(9 * width, offsets_count)
    narrow = back.narrow_sums.reshape(2, 2, 2, width)
    return (
        kept.image_out.reshape(image_in.shape),
        back.image_grad.reshape(image_in.shape),
        grads[5],
        offset_grad,
        back.bias_sum[0, :offsets_count],
        grads[4],
        grads[3],
        grads[2],
        grads[1],
        grads[0],
        narrow[:, :, 1],
        narrow[:, :, 0],
        back.wide_sums[:, 1],
        back.wide_sums[:, 0],
    )


def solution(mesh):
    rows, split, both = P(("dp", "mp"), None, None), P("dp", "mp"), P()
    in_specs = (rows, rows, both, both, split, both, both, split, split, split, split, split)
    in_specs += (both,) * 4
    out_specs = (rows, rows, split, both, both, split, split, split, split, split) + (both,) * 4
    return jax.shard_map(
        per_device, mesh=mesh, in_specs=in_specs, out_specs=out_specs, check_vma=False
    )
```

time: 1920 us -> 482 us (0.25)
  blocking collectives: 777 us -> 0 us
  waiting for transfers between devices: 660 us -> 0 us
  Pallas kernels: 0 us -> 441 us
  other arithmetic: 242 us -> 4.47 us
  matrix products: 159 us -> 0 us
  starting transfers between devices: 31.8 us -> 0 us
    psum x18 -> x0, blocking collectives: 732 us -> none  [the longest x6 249 us: moments(): lax.psum(jnp.sum(centred * centred * valid_map, axis=(0, 1)), ('dp', 'mp'))]
    pallas_call x0 -> x2, Pallas kernels: none -> 441 us  [launch(): pl.pallas_call(body, out_shape=flat_out, in_specs=spec_in, out_specs=spec...]
    reduce_scatter x9 -> x0, waiting for transfers between devices: 430 us -> none  [the longest x1 163 us: split_grads(): lax.psum_scatter(term_mid_a, 'dp', scatter_dimension=0, tiled=True)]
    dot_general x21 -> x0, matrix products: 159 us -> none  [the longest x7 59.8 us: times_transposed(): lax.dot_general(left_side, right_side, (((1,), (1,)), ((), ())), preferre...]
    psum x1 -> x0, waiting for transfers between devices: 132 us -> none  [norm_back(): lax.psum((bias_part, gain_part, offset_terms[0], offset_terms[1]), ('dp',...]
    unnamed x22 -> x0, waiting for transfers between devices: 67.6 us -> none
    mul x17 -> x0, other arithmetic: 57.2 us -> none  [the longest x7 38.9 us: sample_columns(): col_weight * window(padded, row_shift + 1, col_shift + 1, height, breadth)]
    reduce_sum x15 -> x1, other arithmetic: 55 us -> 1.34 us  [per_device(): pixels = jnp.sum(heights * widths).astype(f32)]
  transfers between devices with their start and end apart: 27 -> 0, of which waited for: 16 -> 0; matrix products, arithmetic and copies ran while one was open for 20% -> 0% of each run, Pallas kernels for 0% -> 0%
where the time goes in v2:
time: 482 us; the launch traced here: 479 us
  Pallas kernels  441 us (91%)
  local copies, waits for them, and re-layouts  30.5 us (6%)
    pallas_call x2, Pallas kernels, launch(): pl.pallas_call(body, out_shape=flat_out, in_specs=spec_in, out_specs=spec...  441 us
    unnamed x27, local copies, waits for them, and re-layouts  16.1 us

profile of v2, /device:TPU:8, one launch (start us, length us, event | category | flops | bytes accessed | tf_op | source)
XLA Modules:
  0.0 478.5 jit_solution(9315704384348083238)
XLA Ops:
  0.7 1.3 multiply_reduce_fusion
  2.7 1.2 pad_bitcast_fusion.refs_5_
  3.9 0.9 reduce_window_sum.11
  4.8 0.1 convert_reduce_fusion
  4.8 0.8 slice_bitcast_fusion.3
  5.6 0.1 select_reduce_fusion
  5.7 0.7 fusion.4
  7.1 0.6 pad_maximum_fusion.refs_0_.refs_1_
  7.7 0.1 compare_bitcast_fusion
  7.8 0.1 copy.65
  7.9 0.1 copy.64
  8.0 0.1 copy.63
  8.1 0.1 copy.62
  8.2 0.1 copy.61
  8.3 0.1 stack.43
  8.4 0.6 convert_element_type.29.refs_2_.refs_19_
  9.0 0.1 fusion
  9.0 0.1 reshape.110
  9.1 1.3 reshape.101.refs_4_.refs_21_
  10.4 1.3 reshape.100.refs_3_.refs_20_
  11.7 1.1 reshape.102
  12.9 0.9 copy.67.refs_6_.refs_23_
  13.8 1.0 broadcast_in_dim.77.refs_15_.refs_30_
  14.8 192.7 %forward_pass.1 = (bf16[1408,512]{1,0:T(8,128)(2,1)}, bf16[1408,512]{1,0:T(8,128)(2,1)}, bf16[4,2,256,512]{3,2,1,0:T(8,128)(2,1)}, bf16[4,2,576,512]{3,2,1,0:T(8...) custom-call(f32[3]{0:T(128)} %pad_maximum_fusion.refs_0_.refs_1_, ...), custom_call_target="tpu_custom_call" | custom-call | tf_op jit(solution)/shard_map/forward_pass/pallas_call | solution.py:111
  207.5 248.7 %backward_pass.1 = (f32[1,128]{1,0:T(1,128)}, f32[64,512]{1,0:T(8,128)}, f32[576,128]{1,0:T(8,128)}, f32[256,128]{1,0:T(8,128)}, f32[64,512]{1,0:T(8,128)}, /*in...) custom-call(bf16[1024,2048]{1,0:T(8,128)(2,1)} %bitcast.55, ...), custom_call_target="tpu_custom_call" | custom-call | tf_op jit(solution)/shard_map/backward_pass/pallas_call | solution.py:111
  456.2 1.2 slice_bitcast_fusion.1
  457.4 0.8 fusion.3
  458.2 0.6 copy.84
  458.8 0.6 copy.85
  459.4 0.9 fusion.2
  460.3 0.6 copy.82
  460.9 0.6 copy.83
  461.5 1.4 copy.69
  462.9 0.6 reshape.107
  463.5 0.1 slice_bitcast_fusion
  463.6 0.2 copy.70
  463.8 1.0 reshape.108
  464.9 5.1 %copy.94 = bf16[16,64,2048]{2,1,0:T(8,128)(2,1)} copy(bf16[16,64,2048]{2,1,0:T(8,128)(2,1)} %bitcast.56) | data formatting | bytes 8388608
  469.9 1.1 copy-done
  471.0 3.4 copy.95
  474.4 0.7 copy.96
  475.1 0.7 copy.97
  475.8 0.0 copy-done.5
  475.8 0.7 copy.98
  476.5 0.0 copy-done.4
  476.5 0.7 copy.99
  477.1 0.7 copy.100
  477.9 0.7 copy.101
  (18 shorter events, 0.2 us)
Async XLA Ops:
  464.9 6.2 %copy-start = (f32[1024,2048]{1,0:T(8,128)S(1)}, f32[1024,2048]{1,0:T(8,128)}, u32[]{:S(2)}) copy-start(f32[1024,2048]{1,0:T(8,128)} %get-tuple-element.69) | copy-start | bytes 25165828
  471.0 3.4 copy-start.6
  471.0 4.1 copy-start.2
  471.0 4.8 %copy-start.5 = (f32[64,512]{1,0:T(8,128)S(1)}, f32[64,512]{1,0:T(8,128)}, u32[]{:S(2)}) copy-start(f32[64,512]{1,0:T(8,128)} %get-tuple-element.117) | copy-start | bytes 393220
  471.0 5.5 %copy-start.4 = (f32[256,128]{1,0:T(8,128)S(1)}, f32[256,128]{1,0:T(8,128)}, u32[]{:S(2)}) copy-start(f32[256,128]{1,0:T(8,128)} %get-tuple-element.118) | copy-start | bytes 393220
  471.0 6.1 %copy-start.1 = (f32[576,128]{1,0:T(8,128)S(1)}, f32[576,128]{1,0:T(8,128)}, u32[]{:S(2)}) copy-start(f32[576,128]{1,0:T(8,128)} %get-tuple-element.119) | copy-start | bytes 884740
  471.0 6.8 %copy-start.3 = (f32[64,512]{1,0:T(8,128)S(1)}, f32[64,512]{1,0:T(8,128)}, u32[]{:S(2)}) copy-start(f32[64,512]{1,0:T(8,128)} %get-tuple-element.120) | copy-start | bytes 393220
